TPU v7x, 32 devices: a whole 2x2x4 slice. The times are simulated.
32 devices in a mesh: grp: 2 (over x), fac: 16 (over z, y, core).
Axes of the slice: x: 2, y: 2, z: 4, core: 2. Of those that a mesh axis runs over, the one named last changes fastest.
Arguments:
- model_blocks: bfloat16 [1024, 16384], P(('grp', 'fac')), parts along dimension 0, may hold values from -0.01171875 to 0.01171875
- task_owner: int32 [4096, 1], P(('grp', 'fac')), parts along dimension 0, may hold values from 0 to 15; in each aligned block of 128 rows (0 to 127, 128 to 255, ...) at most 16 rows name the same one
- task_block: int32 [4096], P(('grp', 'fac')), parts along dimension 0, may hold values from 0 to 31
- baseline_of_task: int32 [4096], P(('grp', 'fac')), parts along dimension 0, may hold values from 0 to 63
- coords: float32 [4096, 3, 384], P(('grp', 'fac')), parts along dimension 0, may hold values from -2 to 2
- vis_count: int32 [4096], P(('grp', 'fac')), parts along dimension 0, may hold values from 1 to 384, as said below
Outputs:
- model_visibilities: float32 [128, 2, 384], P(('grp', 'fac')), parts along dimension 0
There are 2 independent parts, one for each index of `grp`. A program takes and returns all parts, laid end to end along the dimension named above; each array names one. Nothing has to cross between parts.
Inputs may be any that keep to these rules, and one draw needn't show every extreme that they name: `task_owner`: within the tasks of one device no facet owner is named by more than 16 tasks. `vis_count`: some task has all 384 visibilities live.
All inputs are finite; a program needn't handle non-finite values.
Results may differ from a plain program's by a relative error of at most 0.0033.
Values may be sent and summed in bfloat16 or wider, within the bound.
A program may use at most 64 MiB of HBM per device.

v0:
```python
import math

import jax
import jax.numpy as jnp
from jax import lax
from jax.sharding import PartitionSpec as P

SUB = 64
LAYERS = 2
BL_DEV = 4


def contributions(block_rows, task_coords, live_count):
    group = block_rows.shape[0]
    samples = task_coords.shape[2]
    offsets = jnp.arange(SUB, dtype=jnp.float32) - SUB / 2
    column_arg = -0.5 * math.pi * task_coords[:, 1][:, None, :] * offsets[None, :, None]
    column_basis = jnp.concatenate([jnp.cos(column_arg), jnp.sin(column_arg)], axis=2).astype(
        jnp.bfloat16
    )
    row_arg = -0.5 * math.pi * offsets[None, :, None] * task_coords[:, 0][:, None, :]
    row_real_part = lax.optimization_barrier(jnp.cos(row_arg).astype(jnp.bfloat16)).astype(
        jnp.float32
    )
    row_im = lax.optimization_barrier(jnp.sin(row_arg).astype(jnp.bfloat16)).astype(jnp.float32)
    pixels = block_rows.reshape(group, LAYERS * 2 * SUB, SUB)
    product = jnp.einsum("grm,gmj->grj", pixels, column_basis, preferred_element_type=jnp.float32)
    product = product.reshape(group, LAYERS, 2, SUB, 2 * samples)
    real_rows = product[:, :, 0]
    imag_rows = product[:, :, 1]
    inner_re = real_rows[..., :samples] - imag_rows[..., samples:]
    inner_im = real_rows[..., samples:] + imag_rows[..., :samples]
    row_real_part = row_real_part[:, None]
    row_im = row_im[:, None]
    layer_re = jnp.sum(row_real_part * inner_re - row_im * inner_im, axis=2)
    layer_im = jnp.sum(row_real_part * inner_im + row_im * inner_re, axis=2)
    layer_offsets = 2.0 * jnp.arange(LAYERS, dtype=jnp.float32) - (LAYERS - 1)
    w_phase = -math.pi * task_coords[:, 2][:, None, :] * layer_offsets[None, :, None]
    cosine = jnp.cos(w_phase)
    sines = jnp.sin(w_phase)
    total_re = jnp.sum(cosine * layer_re - sines * layer_im, axis=1)
    total_im = jnp.sum(cosine * layer_im + sines * layer_re, axis=1)
    live_mask = jnp.arange(samples, dtype=jnp.int32)[None, :] < live_count[:, None]
    stacked = jnp.stack([total_re, total_im], axis=1)
    return jnp.where(live_mask[:, None, :], stacked, jnp.zeros_like(stacked))


def grouped(block_rows, task_coords, live_count):
    total_rows = block_rows.shape[0]
    samples = task_coords.shape[2]

    def one_group(inputs):
        return contributions(inputs[0], inputs[1], inputs[2])

    result = lax.map(
        one_group,
        (
            block_rows.reshape(total_rows // 8, 8, block_rows.shape[1]),
            task_coords.reshape(total_rows // 8, 8, 3, samples),
            live_count.reshape(total_rows // 8, 8),
        ),
    )
    return result.reshape(total_rows, 2, samples)


def body(model_blocks, task_owner, task_block, baseline_of_task, coords, vis_count):
    facets = lax.axis_size("fac")
    task_count = task_block.shape[0]
    capacity = max(2, 2 * task_count // facets)
    owner_ids = task_owner[:, 0]
    onehot = (owner_ids[:, None] == jnp.arange(facets, dtype=jnp.int32)[None, :]).astype(jnp.int32)
    slot_rank = jnp.sum((jnp.cumsum(onehot, axis=0) - onehot) * onehot, axis=1)
    requests = jnp.zeros((facets, capacity), jnp.int32).at[owner_ids, slot_rank].set(task_block)
    fetched = lax.all_to_all(
        model_blocks[lax.all_to_all(requests, "fac", split_axis=0, concat_axis=0, tiled=True)],
        "fac",
        split_axis=0,
        concat_axis=0,
        tiled=True,
    )
    block_rows = fetched[owner_ids, slot_rank]
    block_contribution = grouped(block_rows, coords, vis_count)
    partial_value = jax.ops.segment_sum(
        block_contribution, baseline_of_task, num_segments=BL_DEV * facets
    )
    return lax.psum_scatter(partial_value, "fac", scatter_dimension=0, tiled=True)


def solution(mesh):
    placed = (
        P(("grp", "fac"), None),
        P(("grp", "fac"), None),
        P(("grp", "fac")),
        P(("grp", "fac")),
        P(("grp", "fac"), None, None),
        P(("grp", "fac")),
    )
    return jax.shard_map(
        body, mesh=mesh, in_specs=placed, out_specs=P(("grp", "fac"), None, None), check_vma=False
    )
```

profile of v0, /device:TPU:0, one launch (start us, length us, event | category | flops | bytes accessed | tf_op | source)
XLA Modules:
  0.0 531.8 jit_solution(6223702774541459991)
XLA Ops:
  9.0 11.1 %scatter_fusion = s32[16,16]{1,0:T(8,128)S(1)} fusion(s32[16,16]{1,0:T(8,128)S(1)} %broadcast.141, s32[128]{0:T(128)S(1)} %get-tuple-element.116, s32[128]{0:T(128)} %param.10), kind=kCustom, calls=%fused_computation.2 | custom fusion | bytes 2560 | tf_op jit(solution)/shard_map/scatter | solution.py:73
  20.2 13.6 %all_to_all.17 = s32[16,1,16]{2,1,0:T(1,128)S(1)} all-to-all(s32[16,1,16]{2,1,0:T(1,128)S(1)} %bitcast.69), channel_id=1, replica_groups=mesh['grp'=2,'fac'=16] {'fac'}, dimensions={0} | all-to-all | bytes 2048 | tf_op jit(solution)/shard_map/all_to_all | solution.py:75
  33.9 9.0 %gather_fusion = bf16[256,16384]{1,0:T(8,128)(2,1)} fusion(bf16[32,16384]{1,0:T(8,128)(2,1)S(1)} %copy-done, s32[1024]{0:T(1024)S(1)} %pad_clamp_fusion), kind=kCustom, calls=%fused_computation | custom fusion | bytes 16778240 | tf_op jit(solution)/shard_map/gather | solution.py:75
  48.1 150.3 %all-to-all-done.1 = bf16[16,16,16384]{2,1,0:T(8,128)(2,1)} async-done(((bf16[16,16,16384]{2,1,0:T(8,128)(2,1)}), bf16[16,16,16384]{2,1,0:T(8,128)(2,1)}, u32[]{:S(2)}, u32[]{:S(2)}) %all-to-all-start.1) | async-done | bytes 8388640 | tf_op jit(solution)/shard_map/all_to_all | solution.py:74
  198.4 12.2 %gather_fusion.1 = bf16[128,16384]{1,0:T(8,128)(2,1)} fusion(bf16[16,16,16384]{2,1,0:T(8,128)(2,1)} %all-to-all-done.1, s32[128]{0:T(128)S(1)} %bitcast.71), kind=kCustom, calls=%fused_computation.1 | custom fusion | bytes 8389632 | tf_op jit(solution)/shard_map/gather | solution.py:81
  210.6 183.9 %while.12 = (s32[]{:T(128)}, f32[16,8,2,384]{3,1,0,2:T(8,128)}, s32[16,8]{1,0:T(8,128)S(1)}, f32[16,8,3,384]{3,1,0,2:T(8,128)}, bf16[16,8,16384]{2,1,0:T(8,128)(2,1)}, /*index=5*/s32[]{:T(128)}) while((s32[]{:T(128)}, f32[16,8,2,384]{3,1,0,2:T(8,128)}, s32[16,8]{1,0:T(8,128)S(1)}, f32[16,8,3,384]{3,1,0,2:T(8,128)}, ...), condition=%wide.region_8.9_spmd, body=%wide.region_3.8_spmd.sunk | while | flops 208463040 | bytes 33132224 | solution.py:55
  211.5 5.7 %fusion.38 = (bf16[8,64,384]{2,1,0:T(8,128)(2,1)S(1)}, bf16[8,64,384]{2,1,0:T(8,128)(2,1)S(1)}, bf16[8,64,384]{2,1,0:T(8,128)(2,1)S(1)}, bf16[8,64,384]{2,1,0:T(8,128)(2,1)S(1)}) fusion(f32[8,384]{1,0:T(8,128)S(1)} %get-tuple-element.173, f32[64]{0:T(128)S(1)} %broadcast_multiply_fusion.2, f32[64]{0:T(128)S(1)} %iota_add_fusion.2, ...), kind=kLoop, calls=%fused_computation.14.clone.1 | loop fusion | flops 1179648 | bytes 1597952 | tf_op jit(solution)/shard_map/while/body/eval_jaxpr/convert_element_type | solution.py:22
  222.9 5.7 %fusion.38 = (bf16[8,64,384]{2,1,0:T(8,128)(2,1)S(1)}, bf16[8,64,384]{2,1,0:T(8,128)(2,1)S(1)}, bf16[8,64,384]{2,1,0:T(8,128)(2,1)S(1)}, bf16[8,64,384]{2,1,0:T(8,128)(2,1)S(1)}) fusion(f32[8,384]{1,0:T(8,128)S(1)} %get-tuple-element.173, f32[64]{0:T(128)S(1)} %broadcast_multiply_fusion.2, f32[64]{0:T(128)S(1)} %iota_add_fusion.2, ...), kind=kLoop, calls=%fused_computation.14.clone.1 | loop fusion | flops 1179648 | bytes 1597952 | tf_op jit(solution)/shard_map/while/body/eval_jaxpr/convert_element_type | solution.py:22
  234.4 5.7 %fusion.38 = (bf16[8,64,384]{2,1,0:T(8,128)(2,1)S(1)}, bf16[8,64,384]{2,1,0:T(8,128)(2,1)S(1)}, bf16[8,64,384]{2,1,0:T(8,128)(2,1)S(1)}, bf16[8,64,384]{2,1,0:T(8,128)(2,1)S(1)}) fusion(f32[8,384]{1,0:T(8,128)S(1)} %get-tuple-element.173, f32[64]{0:T(128)S(1)} %broadcast_multiply_fusion.2, f32[64]{0:T(128)S(1)} %iota_add_fusion.2, ...), kind=kLoop, calls=%fused_computation.14.clone.1 | loop fusion | flops 1179648 | bytes 1597952 | tf_op jit(solution)/shard_map/while/body/eval_jaxpr/convert_element_type | solution.py:22
  245.9 5.7 %fusion.38 = (bf16[8,64,384]{2,1,0:T(8,128)(2,1)S(1)}, bf16[8,64,384]{2,1,0:T(8,128)(2,1)S(1)}, bf16[8,64,384]{2,1,0:T(8,128)(2,1)S(1)}, bf16[8,64,384]{2,1,0:T(8,128)(2,1)S(1)}) fusion(f32[8,384]{1,0:T(8,128)S(1)} %get-tuple-element.173, f32[64]{0:T(128)S(1)} %broadcast_multiply_fusion.2, f32[64]{0:T(128)S(1)} %iota_add_fusion.2, ...), kind=kLoop, calls=%fused_computation.14.clone.1 | loop fusion | flops 1179648 | bytes 1597952 | tf_op jit(solution)/shard_map/while/body/eval_jaxpr/convert_element_type | solution.py:22
  257.4 5.7 %fusion.38 = (bf16[8,64,384]{2,1,0:T(8,128)(2,1)S(1)}, bf16[8,64,384]{2,1,0:T(8,128)(2,1)S(1)}, bf16[8,64,384]{2,1,0:T(8,128)(2,1)S(1)}, bf16[8,64,384]{2,1,0:T(8,128)(2,1)S(1)}) fusion(f32[8,384]{1,0:T(8,128)S(1)} %get-tuple-element.173, f32[64]{0:T(128)S(1)} %broadcast_multiply_fusion.2, f32[64]{0:T(128)S(1)} %iota_add_fusion.2, ...), kind=kLoop, calls=%fused_computation.14.clone.1 | loop fusion | flops 1179648 | bytes 1597952 | tf_op jit(solution)/shard_map/while/body/eval_jaxpr/convert_element_type | solution.py:22
  268.9 5.7 %fusion.38 = (bf16[8,64,384]{2,1,0:T(8,128)(2,1)S(1)}, bf16[8,64,384]{2,1,0:T(8,128)(2,1)S(1)}, bf16[8,64,384]{2,1,0:T(8,128)(2,1)S(1)}, bf16[8,64,384]{2,1,0:T(8,128)(2,1)S(1)}) fusion(f32[8,384]{1,0:T(8,128)S(1)} %get-tuple-element.173, f32[64]{0:T(128)S(1)} %broadcast_multiply_fusion.2, f32[64]{0:T(128)S(1)} %iota_add_fusion.2, ...), kind=kLoop, calls=%fused_computation.14.clone.1 | loop fusion | flops 1179648 | bytes 1597952 | tf_op jit(solution)/shard_map/while/body/eval_jaxpr/convert_element_type | solution.py:22
  280.4 5.7 %fusion.38 = (bf16[8,64,384]{2,1,0:T(8,128)(2,1)S(1)}, bf16[8,64,384]{2,1,0:T(8,128)(2,1)S(1)}, bf16[8,64,384]{2,1,0:T(8,128)(2,1)S(1)}, bf16[8,64,384]{2,1,0:T(8,128)(2,1)S(1)}) fusion(f32[8,384]{1,0:T(8,128)S(1)} %get-tuple-element.173, f32[64]{0:T(128)S(1)} %broadcast_multiply_fusion.2, f32[64]{0:T(128)S(1)} %iota_add_fusion.2, ...), kind=kLoop, calls=%fused_computation.14.clone.1 | loop fusion | flops 1179648 | bytes 1597952 | tf_op jit(solution)/shard_map/while/body/eval_jaxpr/convert_element_type | solution.py:22
  291.9 5.7 %fusion.38 = (bf16[8,64,384]{2,1,0:T(8,128)(2,1)S(1)}, bf16[8,64,384]{2,1,0:T(8,128)(2,1)S(1)}, bf16[8,64,384]{2,1,0:T(8,128)(2,1)S(1)}, bf16[8,64,384]{2,1,0:T(8,128)(2,1)S(1)}) fusion(f32[8,384]{1,0:T(8,128)S(1)} %get-tuple-element.173, f32[64]{0:T(128)S(1)} %broadcast_multiply_fusion.2, f32[64]{0:T(128)S(1)} %iota_add_fusion.2, ...), kind=kLoop, calls=%fused_computation.14.clone.1 | loop fusion | flops 1179648 | bytes 1597952 | tf_op jit(solution)/shard_map/while/body/eval_jaxpr/convert_element_type | solution.py:22
  303.4 5.7 %fusion.38 = (bf16[8,64,384]{2,1,0:T(8,128)(2,1)S(1)}, bf16[8,64,384]{2,1,0:T(8,128)(2,1)S(1)}, bf16[8,64,384]{2,1,0:T(8,128)(2,1)S(1)}, bf16[8,64,384]{2,1,0:T(8,128)(2,1)S(1)}) fusion(f32[8,384]{1,0:T(8,128)S(1)} %get-tuple-element.173, f32[64]{0:T(128)S(1)} %broadcast_multiply_fusion.2, f32[64]{0:T(128)S(1)} %iota_add_fusion.2, ...), kind=kLoop, calls=%fused_computation.14.clone.1 | loop fusion | flops 1179648 | bytes 1597952 | tf_op jit(solution)/shard_map/while/body/eval_jaxpr/convert_element_type | solution.py:22
  314.9 5.7 %fusion.38 = (bf16[8,64,384]{2,1,0:T(8,128)(2,1)S(1)}, bf16[8,64,384]{2,1,0:T(8,128)(2,1)S(1)}, bf16[8,64,384]{2,1,0:T(8,128)(2,1)S(1)}, bf16[8,64,384]{2,1,0:T(8,128)(2,1)S(1)}) fusion(f32[8,384]{1,0:T(8,128)S(1)} %get-tuple-element.173, f32[64]{0:T(128)S(1)} %broadcast_multiply_fusion.2, f32[64]{0:T(128)S(1)} %iota_add_fusion.2, ...), kind=kLoop, calls=%fused_computation.14.clone.1 | loop fusion | flops 1179648 | bytes 1597952 | tf_op jit(solution)/shard_map/while/body/eval_jaxpr/convert_element_type | solution.py:22
  326.3 5.7 %fusion.38 = (bf16[8,64,384]{2,1,0:T(8,128)(2,1)S(1)}, bf16[8,64,384]{2,1,0:T(8,128)(2,1)S(1)}, bf16[8,64,384]{2,1,0:T(8,128)(2,1)S(1)}, bf16[8,64,384]{2,1,0:T(8,128)(2,1)S(1)}) fusion(f32[8,384]{1,0:T(8,128)S(1)} %get-tuple-element.173, f32[64]{0:T(128)S(1)} %broadcast_multiply_fusion.2, f32[64]{0:T(128)S(1)} %iota_add_fusion.2, ...), kind=kLoop, calls=%fused_computation.14.clone.1 | loop fusion | flops 1179648 | bytes 1597952 | tf_op jit(solution)/shard_map/while/body/eval_jaxpr/convert_element_type | solution.py:22
  337.8 5.7 %fusion.38 = (bf16[8,64,384]{2,1,0:T(8,128)(2,1)S(1)}, bf16[8,64,384]{2,1,0:T(8,128)(2,1)S(1)}, bf16[8,64,384]{2,1,0:T(8,128)(2,1)S(1)}, bf16[8,64,384]{2,1,0:T(8,128)(2,1)S(1)}) fusion(f32[8,384]{1,0:T(8,128)S(1)} %get-tuple-element.173, f32[64]{0:T(128)S(1)} %broadcast_multiply_fusion.2, f32[64]{0:T(128)S(1)} %iota_add_fusion.2, ...), kind=kLoop, calls=%fused_computation.14.clone.1 | loop fusion | flops 1179648 | bytes 1597952 | tf_op jit(solution)/shard_map/while/body/eval_jaxpr/convert_element_type | solution.py:22
  349.3 5.7 %fusion.38 = (bf16[8,64,384]{2,1,0:T(8,128)(2,1)S(1)}, bf16[8,64,384]{2,1,0:T(8,128)(2,1)S(1)}, bf16[8,64,384]{2,1,0:T(8,128)(2,1)S(1)}, bf16[8,64,384]{2,1,0:T(8,128)(2,1)S(1)}) fusion(f32[8,384]{1,0:T(8,128)S(1)} %get-tuple-element.173, f32[64]{0:T(128)S(1)} %broadcast_multiply_fusion.2, f32[64]{0:T(128)S(1)} %iota_add_fusion.2, ...), kind=kLoop, calls=%fused_computation.14.clone.1 | loop fusion | flops 1179648 | bytes 1597952 | tf_op jit(solution)/shard_map/while/body/eval_jaxpr/convert_element_type | solution.py:22
  360.8 5.7 %fusion.38 = (bf16[8,64,384]{2,1,0:T(8,128)(2,1)S(1)}, bf16[8,64,384]{2,1,0:T(8,128)(2,1)S(1)}, bf16[8,64,384]{2,1,0:T(8,128)(2,1)S(1)}, bf16[8,64,384]{2,1,0:T(8,128)(2,1)S(1)}) fusion(f32[8,384]{1,0:T(8,128)S(1)} %get-tuple-element.173, f32[64]{0:T(128)S(1)} %broadcast_multiply_fusion.2, f32[64]{0:T(128)S(1)} %iota_add_fusion.2, ...), kind=kLoop, calls=%fused_computation.14.clone.1 | loop fusion | flops 1179648 | bytes 1597952 | tf_op jit(solution)/shard_map/while/body/eval_jaxpr/convert_element_type | solution.py:22
  372.3 5.7 %fusion.38 = (bf16[8,64,384]{2,1,0:T(8,128)(2,1)S(1)}, bf16[8,64,384]{2,1,0:T(8,128)(2,1)S(1)}, bf16[8,64,384]{2,1,0:T(8,128)(2,1)S(1)}, bf16[8,64,384]{2,1,0:T(8,128)(2,1)S(1)}) fusion(f32[8,384]{1,0:T(8,128)S(1)} %get-tuple-element.173, f32[64]{0:T(128)S(1)} %broadcast_multiply_fusion.2, f32[64]{0:T(128)S(1)} %iota_add_fusion.2, ...), kind=kLoop, calls=%fused_computation.14.clone.1 | loop fusion | flops 1179648 | bytes 1597952 | tf_op jit(solution)/shard_map/while/body/eval_jaxpr/convert_element_type | solution.py:22
  383.8 5.7 %fusion.38 = (bf16[8,64,384]{2,1,0:T(8,128)(2,1)S(1)}, bf16[8,64,384]{2,1,0:T(8,128)(2,1)S(1)}, bf16[8,64,384]{2,1,0:T(8,128)(2,1)S(1)}, bf16[8,64,384]{2,1,0:T(8,128)(2,1)S(1)}) fusion(f32[8,384]{1,0:T(8,128)S(1)} %get-tuple-element.173, f32[64]{0:T(128)S(1)} %broadcast_multiply_fusion.2, f32[64]{0:T(128)S(1)} %iota_add_fusion.2, ...), kind=kLoop, calls=%fused_computation.14.clone.1 | loop fusion | flops 1179648 | bytes 1597952 | tf_op jit(solution)/shard_map/while/body/eval_jaxpr/convert_element_type | solution.py:22
  395.9 5.5 %scatter_fusion.1 = f32[64,2,384]{2,1,0:T(2,128)S(1)} fusion(f32[64,2,384]{2,1,0:T(2,128)S(1)} %broadcast_in_dim.13, s32[128]{0:T(128)S(1)} %copy-done.2, f32[128,2,384]{2,1,0:T(2,128)S(1)} %copy.44), kind=kCustom, calls=%fused_computation.3 | custom fusion | flops 98304 | bytes 1180160 | tf_op jit(solution)/shard_map/scatter-add | solution.py:83
  403.3 120.4 %all-reduce.3.cloned.1.call-done = f32[64,2,384]{2,1,0:T(2,128)} async-done(((f32[64,2,384]{2,1,0:T(2,128)}), f32[64,2,384]{2,1,0:T(2,128)}) %all-reduce.3.cloned.1.call-update) | async-done | bytes 196624
  (283 shorter events, 102.6 us)
Async XLA Ops:
  6.5 27.3 %copy-start = (bf16[32,16384]{1,0:T(8,128)(2,1)S(1)}, bf16[32,16384]{1,0:T(8,128)(2,1)}, u32[]{:S(2)}) copy-start(bf16[32,16384]{1,0:T(8,128)(2,1)} %param.8) | copy-start | bytes 3145732
  42.9 5.1 copy-start.3
  42.9 155.5 %all-to-all-start.1 = ((bf16[16,16,16384]{2,1,0:T(8,128)(2,1)}), bf16[16,16,16384]{2,1,0:T(8,128)(2,1)}, u32[]{:S(2)}, u32[]{:S(2)}) async-start(bf16[16,16,16384]{2,1,0:T(8,128)(2,1)} %bitcast.70), calls=%async_computation.1 | async-start | bytes 16777216 | tf_op jit(solution)/shard_map/all_to_all | solution.py:74
  47.8 475.9 %all-reduce.3.cloned.1.call-start = ((), (), s32[]{:S(2)}) async-start(), calls=%async_computation.2 | async-start | bytes 393216
  210.6 185.2 %copy-start.2 = (s32[128]{0:T(128)S(1)}, s32[128]{0:T(128)}, u32[]{:S(2)}) copy-start(s32[128]{0:T(128)} %param.11) | copy-start | bytes 1540
  210.6 191.4 %copy-start.4 = (u32[32]{0:T(128)S(1)}, u32[32]{0:T(128)}, u32[]{:S(2)}) copy-start(u32[32]{0:T(128)} %constant.100) | copy-start | bytes 388
  401.3 0.7 copy-start.1
Sparse Core Ops, SparseCore 0:
  402.2 121.4 all-reduce.2
where the time goes:
time: 534 us; the launch traced here: 532 us
  waiting for transfers between devices  271 us (51%)
  other arithmetic  128 us (24%)
  local copies, waits for them, and re-layouts  84 us (16%)
  matrix products  15.2 us (3%)
  between operations  14.2 us (3%)
  blocking collectives  13.6 us (3%)
    all_to_all x1, waiting for transfers between devices, body(): lax.all_to_all(model_blocks[lax.all_to_all(requests, 'fac', split_axis=0,...  150 us
    unnamed x2, waiting for transfers between devices  120 us
    convert_element_type x16, other arithmetic, contributions(): jnp.cos(row_arg).astype(jnp.bfloat16)  91.9 us
    dynamic_slice x16, local copies, waits for them, and re-layouts, grouped(): lax.map(one_group, (block_rows.reshape(total_rows // 8, 8, block_rows.sha...  15.6 us
    dot_general x16, matrix products, contributions(): jnp.einsum('grm,gmj->grj', pixels, column_basis, preferred_element_type=j...  15.2 us
    all_to_all x1, blocking collectives, body(): lax.all_to_all(requests, 'fac', split_axis=0, concat_axis=0, tiled=True)  13.6 us
    squeeze x16, local copies, waits for them, and re-layouts, grouped(): lax.map(one_group, (block_rows.reshape(total_rows // 8, 8, block_rows.sha...  12.4 us
    gather x1, local copies, waits for them, and re-layouts, body(): block_rows = fetched[owner_ids, slot_rank]  12.2 us
  transfers between devices with their start and end apart: 2, of which 2 were waited for; matrix products, arithmetic and copies ran while one was open for 0% of the time, Pallas kernels for 0%

commit v1 on v0

v1 whole, which is shorter than its diff:
```python
import functools
import math

import jax
import jax.numpy as jnp
import numpy as np
from jax import lax
from jax.experimental import pallas as pl
from jax.experimental.pallas import tpu as pltpu
from jax.sharding import PartitionSpec as P

SUB = 64
HALF = SUB // 2
LAYERS = 2
BL_DEV = 4
GROUP = 16
META = 128


def fold_blocks(model_blocks):
    blocks = model_blocks.shape[0]
    pixels = model_blocks.reshape(blocks * LAYERS * 2 * SUB, SUB)
    fold = np.zeros((SUB, SUB), np.float32)
    for n in range(HALF):
        fold[HALF + n, n] = fold[HALF - 1 - n, n] = 1.0
        fold[HALF + n, HALF + n], fold[HALF - 1 - n, HALF + n] = 1.0, -1.0
    fold = jnp.asarray(fold, jnp.bfloat16)
    x = jnp.dot(pixels, fold, preferred_element_type=jnp.float32)
    x = x.reshape(blocks, LAYERS, 2, SUB, SUB)
    plus, minus = x[:, 0] + x[:, 1], x[:, 0] - x[:, 1]
    x = jnp.stack([plus, minus], axis=1)
    upper, lower = x[:, :, :, HALF:], x[:, :, :, HALF - 1 :: -1]
    even, odd = upper + lower, upper - lower

    def parts(rows, turn):
        out_re, out_im = [], []
        for k in range(2):
            for m in range(2):
                re = rows[:, k, 0, :, m * HALF : (m + 1) * HALF]
                im = rows[:, k, 1, :, m * HALF : (m + 1) * HALF]
                times = (k - m + turn) % 4
                for _ in range(times):
                    re, im = -im, re
                out_re.append(re)
                out_im.append(im)
        return jnp.concatenate(out_re, axis=2), jnp.concatenate(out_im, axis=2)

    even_re, even_im = parts(even, 0)
    odd_re, odd_im = parts(odd, 3)
    return jnp.concatenate([even_re, even_im, odd_re, odd_im], axis=1).astype(jnp.bfloat16)


def sincos(x):
    n = jnp.floor(x + 0.5)
    t = (x - n) * (0.5 * math.pi)
    t2 = t * t
    s = t * (1.0 + t2 * (-1.0 / 6 + t2 * (1.0 / 120 + t2 * (-1.0 / 5040 + t2 * (1.0 / 362880)))))
    c = 1.0 + t2 * (-0.5 + t2 * (1.0 / 24 + t2 * (-1.0 / 720 + t2 * (1.0 / 40320 - t2 * (1.0 / 3628800)))))
    turn = n.astype(jnp.int32)
    swap = (turn & 1) == 1
    sine = jnp.where(swap, c, s)
    cosine = jnp.where(swap, s, c)
    sine = jnp.where((turn & 2) == 2, -sine, sine)
    cosine = jnp.where(((turn + 1) & 2) == 2, -cosine, cosine)
    return sine, cosine


def powers(x, cos_ref, sin_ref):
    s0, c0 = sincos(0.5 * x)
    s1, c1 = 2.0 * s0 * c0, 1.0 - 2.0 * s0 * s0
    s, c = s0, c0
    lanes = x.shape[1] // 128
    for p in range(HALF):
        for a in range(lanes):
            cos_ref[a, pl.ds(p, GROUP, stride=HALF), :] = c[:, a * 128 : (a + 1) * 128]
            sin_ref[a, pl.ds(p, GROUP, stride=HALF), :] = s[:, a * 128 : (a + 1) * 128]
        if p < HALF - 1:
            s, c = s * c1 + c * s1, c * c1 - s * s1
    return s0, c0


def load(ref, t):
    lanes = ref.shape[0]
    return jnp.concatenate([ref[a, pl.ds(t * HALF, HALF), :] for a in range(lanes)], axis=1)


def compute_kernel(block_ids, baselines, slots_ref, folded_ref, out_ref, ru, su, rv, sv, cw_ref, sw_ref, sums):
    g = pl.program_id(0)
    vis = out_ref.shape[1] // 2

    @pl.when(g == 0)
    def _():
        out_ref[...] = jnp.zeros_like(out_ref)

    u, v, w = (slots_ref[:, i * vis : (i + 1) * vis] for i in range(3))
    us, uc = powers(u, ru, su)
    vs, vc = powers(v, rv, sv)
    ws, wc = sincos(2.0 * w)
    cw_ref[...] = wc
    sw_ref[...] = ws
    for t in range(GROUP):
        c, s = load(rv, t), load(sv, t)
        cw, sw = cw_ref[t : t + 1, :], sw_ref[t : t + 1, :]
        basis = jnp.concatenate([c * cw, s * cw, c * sw, s * sw], axis=0).astype(jnp.bfloat16)
        inner = jnp.dot(folded_ref[block_ids[g * GROUP + t]], basis, preferred_element_type=jnp.float32)
        rc, rs = load(ru, t), load(su, t)
        re = jnp.sum(rc * inner[:HALF] + rs * inner[2 * HALF : 3 * HALF], axis=0, keepdims=True)
        im = jnp.sum(rc * inner[HALF : 2 * HALF] + rs * inner[3 * HALF :], axis=0, keepdims=True)
        sums[t : t + 1, :vis] = re
        sums[t : t + 1, vis:] = im
    hc, hs = uc * vc - us * vs, uc * vs + us * vc
    re, im = sums[:, :vis], sums[:, vis:]
    live = lax.broadcasted_iota(jnp.int32, (GROUP, vis), 1).astype(jnp.float32) < slots_ref[:, 3 * vis : 3 * vis + 1]
    sums[:, :vis] = jnp.where(live, re * hc - im * hs, 0.0)
    sums[:, vis:] = jnp.where(live, re * hs + im * hc, 0.0)
    for t in range(GROUP):
        b = baselines[g * GROUP + t]
        out_ref[pl.ds(b, 1), :] += sums[t : t + 1, :]


def compute(slots, block_ids, baselines, folded, n_baselines, vis):
    n, width = slots.shape
    lanes = vis // 128
    table = pltpu.VMEM((lanes, GROUP * HALF, 128), jnp.float32)
    return pl.pallas_call(
        compute_kernel,
        out_shape=jax.ShapeDtypeStruct((n_baselines, 2 * vis), jnp.float32),
        grid_spec=pltpu.PrefetchScalarGridSpec(
            num_scalar_prefetch=2,
            grid=(n // GROUP,),
            in_specs=[
                pl.BlockSpec((GROUP, width), lambda g, *_: (g, 0)),
                pl.BlockSpec(folded.shape, lambda g, *_: (0, 0, 0)),
            ],
            out_specs=pl.BlockSpec((n_baselines, 2 * vis), lambda g, *_: (0, 0)),
            scratch_shapes=[
                table,
                table,
                table,
                table,
                pltpu.VMEM((GROUP, vis), jnp.float32),
                pltpu.VMEM((GROUP, vis), jnp.float32),
                pltpu.VMEM((GROUP, 2 * vis), jnp.float32),
            ],
        ),
        compiler_params=pltpu.CompilerParams(vmem_limit_bytes=32 * 1024 * 1024),
        cost_estimate=pl.CostEstimate(flops=n * 128 * 128 * 768, bytes_accessed=4 * n * width, transcendentals=0),
    )(block_ids, baselines, slots, folded)


def body(model_blocks, task_owner, task_block, baseline_of_task, coords, vis_count):
    facets = lax.axis_size("fac")
    tasks, _, vis = coords.shape
    capacity = max(2, 2 * tasks // facets)
    slots = facets * capacity
    owner = task_owner[:, 0]
    same = owner[:, None] == owner[None, :]
    before = jnp.arange(tasks)[None, :] < jnp.arange(tasks)[:, None]
    rank = jnp.sum((same & before).astype(jnp.int32), axis=1)
    slot = owner * capacity + rank
    hit = jnp.arange(slots, dtype=jnp.int32)[:, None] == slot[None, :]
    source = jnp.sum(jnp.where(hit, jnp.arange(tasks, dtype=jnp.int32)[None, :], 0), axis=1)
    meta = jnp.stack([vis_count, task_block, baseline_of_task], axis=1)
    meta = jnp.sum(jnp.where(hit[:, :, None], meta[None], 0), axis=1).astype(jnp.float32)
    meta = jnp.pad(meta, ((0, 0), (0, META - 3)))
    rows = coords.reshape(tasks, 3 * vis)[source]
    sent = jnp.concatenate([rows, meta], axis=1)
    sent = sent.reshape(facets, capacity, 3 * vis + META)
    got = lax.all_to_all(sent, "fac", split_axis=0, concat_axis=0, tiled=True).reshape(slots, 3 * vis + META)
    folded = fold_blocks(model_blocks)
    block_ids = got[:, 3 * vis + 1].astype(jnp.int32)
    baselines = got[:, 3 * vis + 2].astype(jnp.int32)
    partial = compute(got, block_ids, baselines, folded, BL_DEV * facets, vis)
    shares = partial.reshape(facets, BL_DEV, 2 * vis)
    shares = lax.all_to_all(shares, "fac", split_axis=0, concat_axis=0, tiled=True)
    return jnp.sum(shares, axis=0).reshape(BL_DEV, 2, vis)


def solution(mesh):
    placed = (
        P(("grp", "fac"), None),
        P(("grp", "fac"), None),
        P(("grp", "fac")),
        P(("grp", "fac")),
        P(("grp", "fac"), None, None),
        P(("grp", "fac")),
    )
    return jax.shard_map(
        body, mesh=mesh, in_specs=placed, out_specs=P(("grp", "fac"), None, None), check_vma=False
    )
```

time: 534 us -> 112 us (0.21)
  waiting for transfers between devices: 271 us -> 9.43 us
  other arithmetic: 128 us -> 11.8 us
  local copies, waits for them, and re-layouts: 84 us -> 12.4 us
  Pallas kernels: 0 us -> 53.3 us
  matrix products: 15.2 us -> 0.68 us
  between operations: 14.2 us -> 0.2 us
    all_to_all x1, waiting for transfers between devices: 150 us -> 9.43 us  [body(): lax.all_to_all(sent, 'fac', split_axis=0, concat_axis=0, tiled=True)]
    unnamed x2 -> x0, waiting for transfers between devices: 120 us -> none
    convert_element_type x49 -> x2, other arithmetic: 94.6 us -> 0.25 us  [the longest x1 0.25 us: body(): baselines = got[:, 3 * vis + 2].astype(jnp.int32)]
    pallas_call x0 -> x1, Pallas kernels: none -> 53.3 us  [compute(): pl.pallas_call(compute_kernel, out_shape=jax.ShapeDtypeStruct((n_baseline...]
    squeeze x32 -> x1, local copies, waits for them, and re-layouts: 23.2 us -> 0.66 us  [parts(): im = rows[:, k, 1, :, m * HALF:(m + 1) * HALF]]
    gather x2 -> x1, local copies, waits for them, and re-layouts: 21.3 us -> 1.22 us  [body(): rows = coords.reshape(tasks, 3 * vis)[source]]
    dynamic_slice x16 -> x0, local copies, waits for them, and re-layouts: 15.6 us -> none  [grouped(): lax.map(one_group, (block_rows.reshape(total_rows // 8, 8, block_rows.sha...]
    dot_general x16 -> x1, matrix products: 15.2 us -> 0.68 us  [fold_blocks(): x = jnp.dot(pixels, fold, preferred_element_type=jnp.float32)]
  transfers between devices with their start and end apart: 2 -> 1, of which waited for: 2 -> 1; matrix products, arithmetic and copies ran while one was open for 0% -> 15% of each run, Pallas kernels for 0% -> 0%
where the time goes in v1:
time: 112 us
  Pallas kernels  53.3 us (48%)
  blocking collectives  16.8 us (15%)
  local copies, waits for them, and re-layouts  12.4 us (11%)
  other arithmetic  11.8 us (11%)
  waiting for transfers between devices  9.43 us (8%)
  starting transfers between devices  7.39 us (7%)
    pallas_call x1, Pallas kernels, compute(): pl.pallas_call(compute_kernel, out_shape=jax.ShapeDtypeStruct((n_baseline...  53.3 us
    all_to_all x1, blocking collectives, body(): lax.all_to_all(shares, 'fac', split_axis=0, concat_axis=0, tiled=True)  16.8 us
    all_to_all x1, waiting for transfers between devices, body(): lax.all_to_all(sent, 'fac', split_axis=0, concat_axis=0, tiled=True)  9.43 us
    all_to_all x1, starting transfers between devices, body(): lax.all_to_all(sent, 'fac', split_axis=0, concat_axis=0, tiled=True)  7.39 us
    rev x1, local copies, waits for them, and re-layouts, fold_blocks(): upper, lower = (x[:, :, :, HALF:], x[:, :, :, HALF - 1::-1])  3.78 us
    dot_general x1, local copies, waits for them, and re-layouts, fold_blocks(): x = jnp.dot(pixels, fold, preferred_element_type=jnp.float32)  3.04 us
    another operation x1, other arithmetic  2.95 us
    unnamed x12, local copies, waits for them, and re-layouts  2.8 us
  transfers between devices with their start and end apart: 1, of which 1 were waited for; matrix products, arithmetic and copies ran while one was open for 15% of the time, Pallas kernels for 0%

profile of v1, /device:TPU:0, one launch (start us, length us, event | category | flops | bytes accessed | tf_op | source)
XLA Modules:
  0.0 112.0 jit_solution(11616068322713988226)
XLA Ops:
  0.0 0.9 convert_reduce_fusion
  0.9 0.7 multiply_add_fusion
  1.8 1.3 %copy.19 = f32[128,3,384]{0,2,1:T(8,128)S(1)} copy(f32[128,3,384]{2,0,1:T(8,128)} %param.11) | data formatting | bytes 1179648 | tf_op args[4]
  3.0 0.2 copy.20
  3.3 0.2 select_reduce_fusion
  3.5 0.1 copy.26
  3.7 1.2 %gather_fusion = f32[256,1152]{1,0:T(8,128)S(1)} fusion(f32[128,1152]{1,0:T(8,128)S(1)} %copy.20, s32[1024]{0:T(1024)S(1)} %pad_clamp_fusion), kind=kCustom, calls=%fused_computation | custom fusion | bytes 2360320 | tf_op jit(solution)/shard_map/gather | solution.py:166
  4.9 1.2 %select_maximum_fusion = f32[256,1280]{1,0:T(8,128)} fusion(f32[256,3]{1,0:T(8,128)S(1)} %copy.26, f32[256,1152]{1,0:T(8,128)S(1)} %gather_fusion), kind=kLoop, calls=%fused_computation.9 | loop fusion | flops 983040 | bytes 2493440 | tf_op jit(solution)/shard_map/concatenate | solution.py:167
  6.1 7.4 %all-to-all-start = ((f32[16,16,1280]{2,1,0:T(8,128)}), f32[16,16,1280]{2,1,0:T(8,128)S(1)}, u32[]{:S(2)}, u32[]{:S(2)}) async-start(f32[16,16,1280]{2,1,0:T(8,128)} %bitcast.7), calls=%async_computation | async-start | bytes 2621440 | tf_op jit(solution)/shard_map/all_to_all | solution.py:169
  13.5 3.0 %dot_general.5 = bf16[32,2,2,64,64]{4,3,2,1,0:T(8,128)(2,1)S(1)} reshape(bf16[32,16384]{1,0:T(8,128)(2,1)} %param.7) | data formatting | bytes 2097152 | tf_op jit(solution)/shard_map/dot_general | solution.py:28
  16.5 0.7 convolution_bitcast_fusion
  17.2 0.8 slice_add_fusion
  18.1 1.3 %copy-done = f32[32,1,2,64,64]{4,3,0,2,1:T(8,128)} copy-done((f32[32,1,2,64,64]{4,3,0,2,1:T(8,128)}, f32[32,1,2,64,64]{4,3,0,2,1:T(8,128)S(1)}, u32[]{:S(2)}) %copy-start) | copy-done | bytes 1048600
  19.4 1.7 %pad_maximum_fusion = f32[32,2,2,32,64]{4,3,0,2,1:T(8,128)} fusion(f32[32,1,2,64,64]{4,3,0,2,1:T(8,128)S(1)} %get-tuple-element.14, f32[32,1,2,64,64]{4,3,0,2,1:T(8,128)S(1)} %get-tuple-element.13), kind=kLoop, calls=%fused_computation.5 | loop fusion | flops 262144 | bytes 3145728 | tf_op jit(solution)/shard_map/stack | solution.py:31
  21.1 3.8 %rev.3 = f32[32,2,2,32,64]{4,3,0,2,1:T(8,128)} reverse(f32[32,2,2,32,64]{4,3,0,2,1:T(8,128)} %pad_maximum_fusion), dimensions={3} | reverse | bytes 2097152 | tf_op jit(solution)/shard_map/rev | solution.py:32
  24.9 2.9 %fusion.19 = (bf16[32,2,2,32,64]{4,3,0,2,1:T(8,128)(2,1)S(1)}, f32[32,2,2,32,64]{4,3,0,2,1:T(8,128)S(1)}, bf16[32,2,2,32,64]{4,3,0,2,1:T(8,128)(2,1)S(1)}, f32[32,2,2,32,64]{4,3,0,2,1:T(8,128)S(1)}) fusion(f32[32,2,2,32,64]{4,3,0,2,1:T(8,128)} %rev.3, f32[32,1,2,64,64]{4,3,0,2,1:T(8,128)} %copy-done, f32[32,1,2,64,64]{4,3,0,2,1:T(8,128)S(1)} %get-tuple-element.13), kind=kLoop, calls=%fused_computation.56 | loop fusion | flops 1572864 | bytes 6291456 | tf_op jit(solution)/shard_map/convert.45
  27.8 0.7 fusion.8
  28.5 0.7 slice_bitcast_fusion.3
  29.1 2.3 %maximum_maximum_fusion.folded_ref = bf16[32,128,128]{2,1,0:T(8,128)(2,1)S(1)} fusion(bf16[32,32,32]{2,1,0:T(8,128)(2,1)S(1)} %get-tuple-element.31, bf16[32,32,32]{2,1,0:T(8,128)(2,1)S(1)} %get-tuple-element.28, bf16[32,32,32]{2,1,0:T(8,128)(2,1)S(1)} %get-tuple-element.33, bf16[32,32,32]{2,1,0:T(8,128)(2,1)S(1)} %get-tuple-element.32, ...), kind=kLoop, calls=%fused_computation.11 | loop fusion | flops 16777216 | bytes 2097152 | tf_op jit(solution)/shard_map/concatenate | solution.py:50
  31.5 9.4 %all-to-all-done = f32[16,16,1280]{2,1,0:T(8,128)S(1)} async-done(((f32[16,16,1280]{2,1,0:T(8,128)}), f32[16,16,1280]{2,1,0:T(8,128)S(1)}, u32[]{:S(2)}, u32[]{:S(2)}) %all-to-all-start) | async-done | bytes 1310752 | tf_op jit(solution)/shard_map/all_to_all | solution.py:169
  40.9 0.3 fusion.16
  41.1 53.3 %shard_map.73 = f32[64,768]{1,0:T(8,128)S(1)} custom-call(s32[256]{0:T(256)S(1)} %get-tuple-element.6.block_ids, s32[256]{0:T(256)S(1)} %get-tuple-element.5.baselines, f32[256,1280]{1,0:T(8,128)S(1)} %bitcast.49, bf16[32,128,128]{2,1,0:T(8,128)(2,1)S(1)} %maximum_maximum_fusion.folded_ref), custom_call_target="tpu_custom_call" | custom-call | flops 3221225472 | bytes 1310720 | tf_op jit(solution)/shard_map/pallas_call | solution.py:125
  94.5 16.8 %all_to_all.10 = f32[16,4,768]{2,1,0:T(4,128)S(1)} all-to-all(f32[16,4,768]{2,1,0:T(4,128)S(1)} %reshape.78), channel_id=1, replica_groups=mesh['grp'=2,'fac'=16] {'fac'}, dimensions={0} | all-to-all | bytes 393216 | tf_op jit(solution)/shard_map/all_to_all | solution.py:175
  111.3 0.6 reshape.79
  (17 shorter events, 0.3 us)
Async XLA Ops:
  0.0 3.3 %copy-start.4 = (s32[128]{0:T(128)S(1)}, s32[128]{0:T(128)}, u32[]{:S(2)}) copy-start(s32[128]{0:T(128)} %param.12) | copy-start | bytes 1540
  0.0 3.3 %copy-start.3 = (s32[128]{0:T(128)S(1)}, s32[128]{0:T(128)}, u32[]{:S(2)}) copy-start(s32[128]{0:T(128)} %param.9) | copy-start | bytes 1540
  0.0 3.3 %copy-start.2 = (s32[128]{0:T(128)S(1)}, s32[128]{0:T(128)}, u32[]{:S(2)}) copy-start(s32[128]{0:T(128)} %param.10) | copy-start | bytes 1540
  6.1 34.8 %all-to-all-start = ((f32[16,16,1280]{2,1,0:T(8,128)}), f32[16,16,1280]{2,1,0:T(8,128)S(1)}, u32[]{:S(2)}, u32[]{:S(2)}) async-start(f32[16,16,1280]{2,1,0:T(8,128)} %bitcast.7), calls=%async_computation | async-start | bytes 2621440 | tf_op jit(solution)/shard_map/all_to_all | solution.py:169
  13.5 3.1 %copy-start.1 = (bf16[64,64,1,1,1]{1,0,2,4,3:T(8,128)(2,1)S(1)}, bf16[64,64,1,1,1]{1,0,2,4,3:T(8,128)(2,1)}, u32[]{:S(2)}) copy-start(bf16[64,64,1,1,1]{1,0,2,4,3:T(8,128)(2,1)} %constant.15) | copy-start | bytes 24580
  18.1 1.4 %copy-start = (f32[32,1,2,64,64]{4,3,0,2,1:T(8,128)}, f32[32,1,2,64,64]{4,3,0,2,1:T(8,128)S(1)}, u32[]{:S(2)}) copy-start(f32[32,1,2,64,64]{4,3,0,2,1:T(8,128)S(1)} %get-tuple-element.14) | copy-start | bytes 3145732

commit v2 on v1

--- a/solution.py
+++ b/solution.py
@@ -15,6 +15,8 @@
 BL_DEV = 4
 GROUP = 16
 META = 128
+PITCH = 40
+MESH = pl.DeviceIdType.MESH
 
 
 def fold_blocks(model_blocks):
@@ -72,8 +74,8 @@
     lanes = x.shape[1] // 128
     for p in range(HALF):
         for a in range(lanes):
-            cos_ref[a, pl.ds(p, GROUP, stride=HALF), :] = c[:, a * 128 : (a + 1) * 128]
-            sin_ref[a, pl.ds(p, GROUP, stride=HALF), :] = s[:, a * 128 : (a + 1) * 128]
+            cos_ref[a, pl.ds(p, GROUP, stride=PITCH), :] = c[:, a * 128 : (a + 1) * 128]
+            sin_ref[a, pl.ds(p, GROUP, stride=PITCH), :] = s[:, a * 128 : (a + 1) * 128]
         if p < HALF - 1:
             s, c = s * c1 + c * s1, c * c1 - s * s1
     return s0, c0
@@ -81,7 +83,7 @@
 
 def load(ref, t):
     lanes = ref.shape[0]
-    return jnp.concatenate([ref[a, pl.ds(t * HALF, HALF), :] for a in range(lanes)], axis=1)
+    return jnp.concatenate([ref[a, pl.ds(t * PITCH, HALF), :] for a in range(lanes)], axis=1)
 
 
 def compute_kernel(block_ids, baselines, slots_ref, folded_ref, out_ref, ru, su, rv, sv, cw_ref, sw_ref, sums):
@@ -121,7 +123,7 @@
 def compute(slots, block_ids, baselines, folded, n_baselines, vis):
     n, width = slots.shape
     lanes = vis // 128
-    table = pltpu.VMEM((lanes, GROUP * HALF, 128), jnp.float32)
+    table = pltpu.VMEM((lanes, GROUP * PITCH, 128), jnp.float32)
     return pl.pallas_call(
         compute_kernel,
         out_shape=jax.ShapeDtypeStruct((n_baselines, 2 * vis), jnp.float32),
@@ -148,6 +150,211 @@
     )(block_ids, baselines, slots, folded)
 
 
+def fold_matrices():
+    one = np.zeros((SUB, SUB), np.float32)
+    for n in range(HALF):
+        one[HALF + n, n] = one[HALF - 1 - n, n] = 1.0
+        one[HALF + n, HALF + n], one[HALF - 1 - n, HALF + n] = 1.0, -1.0
+    by_layer = []
+    for sign in (1.0, -1.0):
+        pair = np.concatenate([one, sign * one], axis=1)
+        zero = np.zeros_like(pair)
+        by_layer.append(np.block([[pair, zero], [zero, pair]]))
+    rows = one.T.reshape(SUB, HALF, 2).transpose(0, 2, 1).reshape(SUB, SUB)
+    rows = np.concatenate([rows, rows], axis=1)
+    return tuple(jnp.asarray(x, jnp.bfloat16) for x in (*by_layer, rows))
+
+
+def fold_one(pixels, right0, right1, left):
+    y = jnp.dot(pixels[:SUB], right0, preferred_element_type=jnp.float32)
+    y = y + jnp.dot(pixels[SUB:], right1, preferred_element_type=jnp.float32)
+    wide = 2 * SUB
+    z = []
+    for c in range(2):
+        part = y[c * HALF : (c + 1) * HALF]
+        part = jnp.concatenate([part[:, :wide], part[:, wide:]], axis=0)
+        high = part.astype(jnp.bfloat16)
+        low = (part - high.astype(jnp.float32)).astype(jnp.bfloat16)
+        z.append(jnp.dot(left, jnp.concatenate([high, low], axis=0), preferred_element_type=jnp.float32))
+    re, im = z
+    term = lax.broadcasted_iota(jnp.int32, (HALF, wide), 1) // HALF
+
+    def pick(a, b, c, d):
+        return jnp.where(term == 0, a, jnp.where(term == 1, b, jnp.where(term == 2, c, d)))
+
+    ere, eim, ore, oim = re[:HALF], im[:HALF], re[HALF:], im[HALF:]
+    rows = [
+        pick(ere, eim, -eim, ere),
+        pick(eim, -ere, ere, eim),
+        pick(oim, -ore, ore, oim),
+        pick(-ore, -oim, oim, -ore),
+    ]
+    return jnp.concatenate(rows, axis=0).astype(jnp.bfloat16)
+
+
+def fused_kernel(
+    n, source, coords_ref, meta_ref, blocks_ref, right0, right1, left, out_ref,
+    send, recv, meta_recv, meta_smem, folded, ru, su, rv, sv, cw_ref, sw_ref, sums, partial, shares,
+    send_sem, recv_sem, meta_send, meta_got, share_send, share_got, local_sem,
+):
+    vis = coords_ref.shape[2]
+    me = lax.axis_index("fac")
+    barrier = pltpu.get_barrier_semaphore()
+
+    def peer_of(d):
+        return lax.rem(me + d, n)
+
+    @pl.loop(1, n)
+    def _(d):
+        pl.semaphore_signal(barrier, inc=1, device_id={"fac": peer_of(d)}, device_id_type=MESH)
+
+    def pack(d, to):
+        peer = peer_of(d)
+        for r in range(GROUP):
+            row = coords_ref[source[peer * GROUP + r]]
+            for i in range(3):
+                to[d, i, r : r + 1, :] = row[i : i + 1]
+
+    pack(0, recv)
+    meta_recv[0] = meta_ref[me]
+
+    @pl.loop(1, n)
+    def _(d):
+        pack(d, send)
+
+    pl.semaphore_wait(barrier, n - 1)
+
+    def meta_copy(d):
+        return pltpu.make_async_remote_copy(
+            src_ref=meta_ref.at[peer_of(d)], dst_ref=meta_recv.at[d], send_sem=meta_send.at[d],
+            recv_sem=meta_got.at[d], device_id={"fac": peer_of(d)}, device_id_type=MESH,
+        )
+
+    def slot_copy(d):
+        return pltpu.make_async_remote_copy(
+            src_ref=send.at[d], dst_ref=recv.at[d], send_sem=send_sem.at[d],
+            recv_sem=recv_sem.at[d], device_id={"fac": peer_of(d)}, device_id_type=MESH,
+        )
+
+    @pl.loop(1, n)
+    def _(d):
+        meta_copy(d).start()
+
+    @pl.loop(1, n)
+    def _(d):
+        slot_copy(d).start()
+
+    @pl.loop(0, blocks_ref.shape[0])
+    def _(b):
+        folded[b] = fold_one(blocks_ref[b], right0[...], right1[...], left[...])
+
+    @pl.loop(1, n)
+    def _(d):
+        meta_copy(d).wait()
+
+    to_scalars = pltpu.make_async_copy(meta_recv, meta_smem, local_sem)
+    to_scalars.start()
+    partial[...] = jnp.zeros_like(partial)
+    to_scalars.wait()
+
+    @pl.loop(0, n)
+    def _(d):
+        @pl.when(d > 0)
+        def _():
+            slot_copy(d).wait()
+
+        us, uc = powers(recv[d, 0], ru, su)
+        vs, vc = powers(recv[d, 1], rv, sv)
+        ws, wc = sincos(2.0 * recv[d, 2])
+        cw_ref[...] = wc
+        sw_ref[...] = ws
+        for t in range(GROUP):
+            c, s = load(rv, t), load(sv, t)
+            cw, sw = cw_ref[t : t + 1, :], sw_ref[t : t + 1, :]
+            basis = jnp.concatenate([c * cw, s * cw, c * sw, s * sw], axis=0).astype(jnp.bfloat16)
+            inner = jnp.dot(folded[meta_smem[d, t, 1]], basis, preferred_element_type=jnp.float32)
+            rc, rs = load(ru, t), load(su, t)
+            re = jnp.sum(rc * inner[:HALF] + rs * inner[2 * HALF : 3 * HALF], axis=0, keepdims=True)
+            im = jnp.sum(rc * inner[HALF : 2 * HALF] + rs * inner[3 * HALF :], axis=0, keepdims=True)
+            sums[t : t + 1, :vis] = re
+            sums[t : t + 1, vis:] = im
+        hc, hs = uc * vc - us * vs, uc * vs + us * vc
+        re, im = sums[:, :vis], sums[:, vis:]
+        meta = meta_recv[d]
+        live = lax.broadcasted_iota(jnp.int32, (GROUP, vis), 1) < meta[:, 0:1]
+        both = jnp.concatenate([re * hc - im * hs, re * hs + im * hc], axis=0)
+        both = jnp.where(jnp.concatenate([live, live], axis=0), both, 0.0)
+        high = both.astype(jnp.bfloat16).astype(jnp.float32)
+        both = jnp.concatenate([high, both - high], axis=0).astype(jnp.bfloat16)
+        baseline = meta[:, 2:3]
+        row = (baseline // BL_DEV) * (2 * BL_DEV) + baseline % BL_DEV
+        row = jnp.concatenate([row, row + BL_DEV, row, row + BL_DEV], axis=0)
+        onehot = lax.broadcasted_iota(jnp.int32, (4 * GROUP, n * 2 * BL_DEV), 1) == row
+        onehot = jnp.where(onehot, 1.0, 0.0).astype(jnp.bfloat16)
+        added = lax.dot_general(onehot, both, (((0,), (0,)), ((), ())), preferred_element_type=jnp.float32)
+        partial[...] += added.reshape(partial.shape)
+
+    def share_copy(d):
+        return pltpu.make_async_remote_copy(
+            src_ref=partial.at[peer_of(d)], dst_ref=shares.at[d], send_sem=share_send.at[d],
+            recv_sem=share_got.at[d], device_id={"fac": peer_of(d)}, device_id_type=MESH,
+        )
+
+    @pl.loop(1, n)
+    def _(d):
+        share_copy(d).start()
+
+    out_ref[...] = partial[me]
+
+    @pl.loop(1, n)
+    def _(d):
+        share_copy(d).wait()
+        out_ref[...] += shares[d]
+
+
+def fused(source, coords, meta, blocks, n):
+    tasks, _, vis = coords.shape
+    table = pltpu.VMEM((vis // 128, GROUP * PITCH, 128), jnp.float32)
+    vmem = pl.BlockSpec(memory_space=pltpu.VMEM)
+    rows = 2 * BL_DEV
+    sems = pltpu.SemaphoreType.DMA((n,))
+    return pl.pallas_call(
+        functools.partial(fused_kernel, n),
+        out_shape=jax.ShapeDtypeStruct((rows, vis), jnp.float32),
+        in_specs=[pl.BlockSpec(memory_space=pltpu.SMEM)] + [vmem] * 6,
+        out_specs=vmem,
+        scratch_shapes=[
+            pltpu.VMEM((n, 3, GROUP, vis), jnp.float32),
+            pltpu.VMEM((n, 3, GROUP, vis), jnp.float32),
+            pltpu.VMEM((n, GROUP, META), jnp.int32),
+            pltpu.SMEM((n, GROUP, META), jnp.int32),
+            pltpu.VMEM((blocks.shape[0], 2 * SUB, 2 * SUB), jnp.bfloat16),
+            table,
+            table,
+            table,
+            table,
+            pltpu.VMEM((GROUP, vis), jnp.float32),
+            pltpu.VMEM((GROUP, vis), jnp.float32),
+            pltpu.VMEM((GROUP, 2 * vis), jnp.float32),
+            pltpu.VMEM((n, rows, vis), jnp.float32),
+            pltpu.VMEM((n, rows, vis), jnp.float32),
+            sems,
+            sems,
+            sems,
+            sems,
+            sems,
+            sems,
+            pltpu.SemaphoreType.DMA,
+        ],
+        compiler_params=pltpu.CompilerParams(
+            collective_id=0, has_side_effects=True, vmem_limit_bytes=40 * 1024 * 1024
+        ),
+        cost_estimate=pl.CostEstimate(
+            flops=n * GROUP * 128 * 128 * 768, bytes_accessed=4 * n * GROUP * 3 * vis, transcendentals=0
+        ),
+    )(source, coords, meta, blocks, *fold_matrices())
+
+
 def body(model_blocks, task_owner, task_block, baseline_of_task, coords, vis_count):
     facets = lax.axis_size("fac")
     tasks, _, vis = coords.shape
@@ -161,8 +368,13 @@
     hit = jnp.arange(slots, dtype=jnp.int32)[:, None] == slot[None, :]
     source = jnp.sum(jnp.where(hit, jnp.arange(tasks, dtype=jnp.int32)[None, :], 0), axis=1)
     meta = jnp.stack([vis_count, task_block, baseline_of_task], axis=1)
-    meta = jnp.sum(jnp.where(hit[:, :, None], meta[None], 0), axis=1).astype(jnp.float32)
+    meta = jnp.sum(jnp.where(hit[:, :, None], meta[None], 0), axis=1)
     meta = jnp.pad(meta, ((0, 0), (0, META - 3)))
+    if capacity == GROUP:
+        blocks = model_blocks.reshape(model_blocks.shape[0], 2 * SUB, 2 * SUB)
+        share = fused(source, coords, meta.reshape(facets, capacity, META), blocks, facets)
+        return share.reshape(2, BL_DEV, vis).transpose(1, 0, 2)
+    meta = meta.astype(jnp.float32)
     rows = coords.reshape(tasks, 3 * vis)[source]
     sent = jnp.concatenate([rows, meta], axis=1)
     sent = sent.reshape(facets, capacity, 3 * vis + META)

time: 112 us -> 58.9 us (0.53)
  blocking collectives: 16.8 us -> 0 us
  waiting for transfers between devices: 9.43 us -> 0 us
  local copies, waits for them, and re-layouts: 12.4 us -> 3.09 us
  other arithmetic: 11.8 us -> 2.62 us
  starting transfers between devices: 7.39 us -> 0 us
    all_to_all x1 -> x0, blocking collectives: 16.8 us -> none  [body(): lax.all_to_all(shares, 'fac', split_axis=0, concat_axis=0, tiled=True)]
    all_to_all x1 -> x0, waiting for transfers between devices: 9.43 us -> none  [body(): lax.all_to_all(sent, 'fac', split_axis=0, concat_axis=0, tiled=True)]
    all_to_all x1 -> x0, starting transfers between devices: 7.39 us -> none  [body(): lax.all_to_all(sent, 'fac', split_axis=0, concat_axis=0, tiled=True)]
    another operation x2 -> x0, other arithmetic: 4.6 us -> none
    rev x1 -> x0, local copies, waits for them, and re-layouts: 3.78 us -> none  [fold_blocks(): upper, lower = (x[:, :, :, HALF:], x[:, :, :, HALF - 1::-1])]
    concatenate x2 -> x0, other arithmetic: 3.49 us -> none  [the longest x1 2.31 us: fold_blocks(): jnp.concatenate([even_re, even_im, odd_re, odd_im], axis=1)]
    dot_general x1 -> x0, local copies, waits for them, and re-layouts: 3.04 us -> none  [fold_blocks(): x = jnp.dot(pixels, fold, preferred_element_type=jnp.float32)]
    gather x1 -> x0, local copies, waits for them, and re-layouts: 1.22 us -> none  [body(): rows = coords.reshape(tasks, 3 * vis)[source]]
  transfers between devices with their start and end apart: 1 -> 0, of which waited for: 1 -> 0; matrix products, arithmetic and copies ran while one was open for 15% -> 0% of each run, Pallas kernels for 0% -> 0%
where the time goes in v2:
time: 58.9 us; the launch traced here: 58.6 us
  Pallas kernels  52.8 us (90%)
  local copies, waits for them, and re-layouts  3.09 us (5%)
  other arithmetic  2.62 us (4%)
    pallas_call x1, Pallas kernels, fused(): pl.pallas_call(functools.partial(fused_kernel, n), out_shape=jax.ShapeDty...  52.8 us
    unnamed x11, local copies, waits for them, and re-layouts  2.46 us

profile of v2, /device:TPU:0, one launch (start us, length us, event | category | flops | bytes accessed | tf_op | source)
XLA Modules:
  0.0 58.6 jit_solution(13629971224171524735)
XLA Ops:
  0.0 0.0 copy-start.3
  0.0 0.9 %convert_reduce_fusion = s32[128]{0:T(128)S(1)} fusion(s32[128]{0:T(128)} %bitcast.17), kind=kLoop, calls=%fused_computation.3 | loop fusion | flops 81792 | bytes 1024 | tf_op jit(solution)/shard_map/reduce_sum | solution.py:366
  0.9 0.7 %multiply_add_fusion = s32[128]{0:T(128)S(1)} fusion(s32[128]{0:T(128)S(1)} %convert_reduce_fusion, s32[128,1]{0,1:T(1,128)} %param.10), kind=kLoop, calls=%fused_computation.8 | loop fusion | flops 256 | bytes 1536 | tf_op jit(solution)/shard_map/add | solution.py:367
  1.6 0.1 select_reduce_fusion.1.source
  1.7 0.7 %pad_add_fusion = s32[128,3]{0,1:T(4,128)S(1)} fusion(s32[128,1]{0,1:T(1,128)} %bitcast.14, s32[128,1]{0,1:T(1,128)} %bitcast.15, s32[128,1]{0,1:T(1,128)} %bitcast.16), kind=kLoop, calls=%fused_computation.7 | loop fusion | flops 768 | bytes 3072 | tf_op jit(solution)/shard_map/stack | solution.py:370
  2.4 0.2 select_reduce_fusion
  2.6 0.1 copy.16
  2.8 1.5 %copy.14.coords_ref = f32[128,3,384]{2,1,0:T(4,128)S(1)} copy(f32[128,3,384]{2,0,1:T(8,128)} %param.13) | data formatting | bytes 1179648 | tf_op args[4]
  4.3 0.0 copy-done.3
  4.3 0.0 copy-start
  4.3 0.0 copy-start.1
  4.3 0.0 copy-start.2
  4.3 0.2 copy.17
  4.6 0.6 copy-done
  5.1 0.0 copy-done.1
  5.2 0.0 copy-done.2
  5.2 52.8 %shard_map.91 = f32[8,384]{1,0:T(8,128)S(1)} custom-call(s32[256]{0:T(256)S(1)} %select_reduce_fusion.1.source, f32[128,3,384]{2,1,0:T(4,128)S(1)} %copy.14.coords_ref, s32[16,16,128]{2,1,0:T(8,128)S(1)} %bitcast.12, bf16[32,128,128]{2,1,0:T(8,128)(2,1)S(1)} %bitcast.11, bf16[128,256]{1,0:T(8,128)(2,1)S(1)} %copy-done.1, bf16[128,256]{1,0:T(8,128)(2,1)S(1)} %copy-done, ...), custom_call_target="tpu_custom_call" | custom-call | flops 3221225472 | bytes 1179648 | tf_op jit(solution)/shard_map/pallas_call | solution.py:321
  58.0 0.6 %copy.19 = f32[2,4,384]{2,0,1:T(2,128)} copy(f32[2,4,384]{2,1,0:T(4,128)S(1)} %reshape.40) | data formatting | bytes 24576 | tf_op jit(solution)/shard_map/reshape | solution.py:376
  (3 shorter events, 0.1 us)
Async XLA Ops:
  0.0 4.3 %copy-start.3 = (bf16[32,16384]{1,0:T(8,128)(2,1)S(1)}, bf16[32,16384]{1,0:T(8,128)(2,1)}, u32[]{:S(2)}) copy-start(bf16[32,16384]{1,0:T(8,128)(2,1)} %param.9) | copy-start | bytes 3145732
  4.3 0.8 %copy-start = (bf16[128,256]{1,0:T(8,128)(2,1)S(1)}, bf16[128,256]{1,0:T(8,128)(2,1)}, u32[]{:S(2)}) copy-start(bf16[128,256]{1,0:T(8,128)(2,1)} %constant.11.clone.right1) | copy-start | bytes 196612
  4.3 0.9 %copy-start.1 = (bf16[128,256]{1,0:T(8,128)(2,1)S(1)}, bf16[128,256]{1,0:T(8,128)(2,1)}, u32[]{:S(2)}) copy-start(bf16[128,256]{1,0:T(8,128)(2,1)} %constant.10.clone.right0) | copy-start | bytes 196612
  4.3 0.9 %copy-start.2 = (bf16[64,128]{1,0:T(8,128)(2,1)S(1)}, bf16[64,128]{1,0:T(8,128)(2,1)}, u32[]{:S(2)}) copy-start(bf16[64,128]{1,0:T(8,128)(2,1)} %constant.12.clone.left) | copy-start | bytes 49156

commit v3 on v2

--- a/solution.py
+++ b/solution.py
@@ -16,6 +16,7 @@
 GROUP = 16
 META = 128
 PITCH = 40
+STEPS = 16383.5
 MESH = pl.DeviceIdType.MESH
 
 
@@ -69,15 +70,15 @@
 
 def powers(x, cos_ref, sin_ref):
     s0, c0 = sincos(0.5 * x)
-    s1, c1 = 2.0 * s0 * c0, 1.0 - 2.0 * s0 * s0
-    s, c = s0, c0
+    twice = 2.0 - 4.0 * s0 * s0
+    s, c, s_last, c_last = s0, c0, -s0, c0
     lanes = x.shape[1] // 128
     for p in range(HALF):
         for a in range(lanes):
             cos_ref[a, pl.ds(p, GROUP, stride=PITCH), :] = c[:, a * 128 : (a + 1) * 128]
             sin_ref[a, pl.ds(p, GROUP, stride=PITCH), :] = s[:, a * 128 : (a + 1) * 128]
         if p < HALF - 1:
-            s, c = s * c1 + c * s1, c * c1 - s * s1
+            s, c, s_last, c_last = twice * s - s_last, twice * c - c_last, s, c
     return s0, c0
 
 
@@ -194,10 +195,12 @@
 
 def fused_kernel(
     n, source, coords_ref, meta_ref, blocks_ref, right0, right1, left, out_ref,
-    send, recv, meta_recv, meta_smem, folded, ru, su, rv, sv, cw_ref, sw_ref, sums, partial, shares,
+    stage, send, recv, meta_recv, meta_smem, folded, ru, su, rv, sv, cw_ref, sw_ref, sums, partial, shares,
     send_sem, recv_sem, meta_send, meta_got, share_send, share_got, local_sem,
 ):
     vis = coords_ref.shape[2]
+    meta_lane = lax.broadcasted_iota(jnp.int32, (GROUP, META), 1)
+    meta_row = lax.broadcasted_iota(jnp.int32, (GROUP, META), 0)
     me = lax.axis_index("fac")
     barrier = pltpu.get_barrier_semaphore()
 
@@ -211,18 +214,13 @@
     def pack(d, to):
         peer = peer_of(d)
         for r in range(GROUP):
-            row = coords_ref[source[peer * GROUP + r]]
+            task = source[peer * GROUP + r]
             for i in range(3):
-                to[d, i, r : r + 1, :] = row[i : i + 1]
+                stage[i, r : r + 1, :] = coords_ref[i, pl.ds(task, 1), :]
+        to[d] = jnp.floor(stage[...] * STEPS + 0.5).astype(jnp.int32).astype(jnp.int16)
 
     pack(0, recv)
     meta_recv[0] = meta_ref[me]
-
-    @pl.loop(1, n)
-    def _(d):
-        pack(d, send)
-
-    pl.semaphore_wait(barrier, n - 1)
 
     def meta_copy(d):
         return pltpu.make_async_remote_copy(
@@ -236,12 +234,15 @@
             recv_sem=recv_sem.at[d], device_id={"fac": peer_of(d)}, device_id_type=MESH,
         )
 
+    pl.semaphore_wait(barrier, n - 1)
+
     @pl.loop(1, n)
     def _(d):
         meta_copy(d).start()
 
     @pl.loop(1, n)
     def _(d):
+        pack(d, send)
         slot_copy(d).start()
 
     @pl.loop(0, blocks_ref.shape[0])
@@ -263,16 +264,17 @@
         def _():
             slot_copy(d).wait()
 
-        us, uc = powers(recv[d, 0], ru, su)
-        vs, vc = powers(recv[d, 1], rv, sv)
-        ws, wc = sincos(2.0 * recv[d, 2])
+        u, v, w = (recv[d, i].astype(jnp.int32).astype(jnp.float32) * (1.0 / STEPS) for i in range(3))
+        us, uc = powers(u, ru, su)
+        vs, vc = powers(v, rv, sv)
+        ws, wc = sincos(2.0 * w)
         cw_ref[...] = wc
         sw_ref[...] = ws
         for t in range(GROUP):
             c, s = load(rv, t), load(sv, t)
             cw, sw = cw_ref[t : t + 1, :], sw_ref[t : t + 1, :]
             basis = jnp.concatenate([c * cw, s * cw, c * sw, s * sw], axis=0).astype(jnp.bfloat16)
-            inner = jnp.dot(folded[meta_smem[d, t, 1]], basis, preferred_element_type=jnp.float32)
+            inner = jnp.dot(folded[meta_smem[d, 0, GROUP + t]], basis, preferred_element_type=jnp.float32)
             rc, rs = load(ru, t), load(su, t)
             re = jnp.sum(rc * inner[:HALF] + rs * inner[2 * HALF : 3 * HALF], axis=0, keepdims=True)
             im = jnp.sum(rc * inner[HALF : 2 * HALF] + rs * inner[3 * HALF :], axis=0, keepdims=True)
@@ -280,16 +282,20 @@
             sums[t : t + 1, vis:] = im
         hc, hs = uc * vc - us * vs, uc * vs + us * vc
         re, im = sums[:, :vis], sums[:, vis:]
-        meta = meta_recv[d]
-        live = lax.broadcasted_iota(jnp.int32, (GROUP, vis), 1) < meta[:, 0:1]
+        meta = meta_recv[d].astype(jnp.float32)
+
+        def column(first):
+            picked = jnp.where(meta_lane == meta_row + first, meta, 0.0)
+            return jnp.sum(picked, axis=1, keepdims=True)
+
+        live = lax.broadcasted_iota(jnp.int32, (GROUP, vis), 1).astype(jnp.float32) < column(0)
         both = jnp.concatenate([re * hc - im * hs, re * hs + im * hc], axis=0)
         both = jnp.where(jnp.concatenate([live, live], axis=0), both, 0.0)
         high = both.astype(jnp.bfloat16).astype(jnp.float32)
         both = jnp.concatenate([high, both - high], axis=0).astype(jnp.bfloat16)
-        baseline = meta[:, 2:3]
-        row = (baseline // BL_DEV) * (2 * BL_DEV) + baseline % BL_DEV
+        row = column(2 * GROUP)
         row = jnp.concatenate([row, row + BL_DEV, row, row + BL_DEV], axis=0)
-        onehot = lax.broadcasted_iota(jnp.int32, (4 * GROUP, n * 2 * BL_DEV), 1) == row
+        onehot = lax.broadcasted_iota(jnp.int32, (4 * GROUP, n * 2 * BL_DEV), 1).astype(jnp.float32) == row
         onehot = jnp.where(onehot, 1.0, 0.0).astype(jnp.bfloat16)
         added = lax.dot_general(onehot, both, (((0,), (0,)), ((), ())), preferred_element_type=jnp.float32)
         partial[...] += added.reshape(partial.shape)
@@ -313,7 +319,7 @@
 
 
 def fused(source, coords, meta, blocks, n):
-    tasks, _, vis = coords.shape
+    vis = coords.shape[2]
     table = pltpu.VMEM((vis // 128, GROUP * PITCH, 128), jnp.float32)
     vmem = pl.BlockSpec(memory_space=pltpu.VMEM)
     rows = 2 * BL_DEV
@@ -324,10 +330,11 @@
         in_specs=[pl.BlockSpec(memory_space=pltpu.SMEM)] + [vmem] * 6,
         out_specs=vmem,
         scratch_shapes=[
-            pltpu.VMEM((n, 3, GROUP, vis), jnp.float32),
-            pltpu.VMEM((n, 3, GROUP, vis), jnp.float32),
-            pltpu.VMEM((n, GROUP, META), jnp.int32),
-            pltpu.SMEM((n, GROUP, META), jnp.int32),
+            pltpu.VMEM((3, GROUP, vis), jnp.float32),
+            pltpu.VMEM((n, 3, GROUP, vis), jnp.int16),
+            pltpu.VMEM((n, 3, GROUP, vis), jnp.int16),
+            pltpu.VMEM((n, 1, META), jnp.int32),
+            pltpu.SMEM((n, 1, META), jnp.int32),
             pltpu.VMEM((blocks.shape[0], 2 * SUB, 2 * SUB), jnp.bfloat16),
             table,
             table,
@@ -367,13 +374,18 @@
     slot = owner * capacity + rank
     hit = jnp.arange(slots, dtype=jnp.int32)[:, None] == slot[None, :]
     source = jnp.sum(jnp.where(hit, jnp.arange(tasks, dtype=jnp.int32)[None, :], 0), axis=1)
+    if capacity == GROUP:
+        row = (baseline_of_task // BL_DEV) * (2 * BL_DEV) + baseline_of_task % BL_DEV
+        meta = jnp.stack([vis_count, task_block, row])
+        meta = jnp.where(hit.reshape(facets, 1, capacity, tasks), meta[None, :, None, :], 0)
+        meta = jnp.sum(meta, axis=3).reshape(facets, 1, 3 * capacity)
+        meta = jnp.pad(meta, ((0, 0), (0, 0), (0, META - 3 * capacity)))
+        blocks = model_blocks.reshape(model_blocks.shape[0], 2 * SUB, 2 * SUB)
+        share = fused(source, coords.transpose(1, 0, 2), meta, blocks, facets)
+        return share.reshape(2, BL_DEV, vis).transpose(1, 0, 2)
     meta = jnp.stack([vis_count, task_block, baseline_of_task], axis=1)
     meta = jnp.sum(jnp.where(hit[:, :, None], meta[None], 0), axis=1)
     meta = jnp.pad(meta, ((0, 0), (0, META - 3)))
-    if capacity == GROUP:
-        blocks = model_blocks.reshape(model_blocks.shape[0], 2 * SUB, 2 * SUB)
-        share = fused(source, coords, meta.reshape(facets, capacity, META), blocks, facets)
-        return share.reshape(2, BL_DEV, vis).transpose(1, 0, 2)
     meta = meta.astype(jnp.float32)
     rows = coords.reshape(tasks, 3 * vis)[source]
     sent = jnp.concatenate([rows, meta], axis=1)

time: 58.9 us -> 51.2 us (0.87)
  Pallas kernels: 52.8 us -> 45.4 us
  other arithmetic: 2.62 us -> 1.33 us
  local copies, waits for them, and re-layouts: 3.09 us -> 4.11 us
    pallas_call x1, Pallas kernels: 52.8 us -> 45.4 us  [fused(): pl.pallas_call(functools.partial(fused_kernel, n), out_shape=jax.ShapeDty...]
    unnamed x11 -> x17, local copies, waits for them, and re-layouts: 2.46 us -> 3.4 us
    reduce_sum x1, other arithmetic: 0.93 us -> 0.17 us  [body(): rank = jnp.sum((same & before).astype(jnp.int32), axis=1)]
    reduce_sum x1, other arithmetic: 0.18 us -> 0.91 us  [body(): meta = jnp.sum(meta, axis=3).reshape(facets, 1, 3 * capacity)]
    another operation x1 -> x2, other arithmetic: 0.7 us -> 0.02 us  [body(): meta = jnp.stack([vis_count, task_block, row])]
    add x1, other arithmetic: 0.67 us -> 0.01 us  [body(): slot = owner * capacity + rank]
where the time goes in v3:
time: 51.2 us; the launch traced here: 51 us
  Pallas kernels  45.4 us (89%)
  local copies, waits for them, and re-layouts  4.11 us (8%)
  other arithmetic  1.33 us (3%)
    pallas_call x1, Pallas kernels, fused(): pl.pallas_call(functools.partial(fused_kernel, n), out_shape=jax.ShapeDty...  45.4 us
    unnamed x17, local copies, waits for them, and re-layouts  3.4 us

profile of v3, /device:TPU:0, one launch (start us, length us, event | category | flops | bytes accessed | tf_op | source)
XLA Modules:
  0.0 51.0 jit_solution(2335743077376157438)
XLA Ops:
  0.0 0.0 copy-start.6
  0.0 0.7 %copy-done.6 = s32[128]{0:T(128)S(1)} copy-done((s32[128]{0:T(128)S(1)}, s32[128]{0:T(128)}, u32[]{:S(2)}) %copy-start.6) | copy-done | bytes 536
  0.7 0.0 copy-start.7
  0.7 0.6 %copy-done.7 = s32[128,1]{0,1:T(1,128)S(1)} copy-done((s32[128,1]{0,1:T(1,128)S(1)}, s32[128,1]{0,1:T(1,128)}, u32[]{:S(2)}) %copy-start.7) | copy-done | bytes 536
  1.3 0.2 convert_reduce_fusion
  1.5 0.0 copy-start.4
  1.5 0.0 copy-start.5
  1.5 0.1 select_reduce_fusion.1.source
  1.6 0.5 %copy-done.4 = s32[128]{0:T(128)S(1)} copy-done((s32[128]{0:T(128)S(1)}, s32[128]{0:T(128)}, u32[]{:S(2)}) %copy-start.4) | copy-done | bytes 536
  2.2 0.0 copy-done.5
  2.2 0.1 broadcast_compare_fusion
  2.3 0.9 %select_reduce_fusion = s32[16,3,16]{2,1,0:T(4,128)S(1)} fusion(s32[3,128]{1,0:T(4,128)S(1)} %pad_add_fusion, pred[16,16,128]{2,1,0:T(8,128)(4,1)S(1)} %broadcast_compare_fusion), kind=kLoop, calls=%fused_computation | loop fusion | flops 195840 | bytes 37376 | tf_op jit(solution)/shard_map/reduce_sum | solution.py:381
  3.2 0.1 reshape.37
  3.3 0.0 copy-start
  3.3 0.0 copy-start.1
  3.3 0.0 copy-start.2
  3.4 0.0 copy-start.3
  3.4 1.5 %copy.15 = bf16[4,8,128,128]{3,2,1,0:T(8,128)(2,1)S(1)} copy(bf16[4,8,128,128]{3,1,2,0:T(8,128)(2,1)} %bitcast.15) | data formatting | bytes 2097152
  4.9 0.0 copy-done
  4.9 0.0 copy-done.1
  4.9 0.0 copy-done.2
  4.9 0.0 copy-done.3
  4.9 45.4 %shard_map.91 = f32[8,384]{1,0:T(8,128)S(1)} custom-call(s32[256]{0:T(256)S(1)} %select_reduce_fusion.1.source, f32[3,128,384]{2,1,0:T(8,128)S(1)} %bitcast.14, s32[16,1,128]{2,1,0:T(1,128)S(1)} %pad.4.meta_ref, bf16[32,128,128]{2,1,0:T(8,128)(2,1)S(1)} %bitcast.13, bf16[128,256]{1,0:T(8,128)(2,1)S(1)} %copy-done.2, bf16[128,256]{1,0:T(8,128)(2,1)S(1)} %copy-done.1, ...), custom_call_target="tpu_custom_call" | custom-call | flops 3221225472 | bytes 1179648 | tf_op jit(solution)/shard_map/pallas_call | solution.py:327
  50.4 0.6 %copy.17 = f32[2,4,384]{2,0,1:T(2,128)} copy(f32[2,4,384]{2,1,0:T(4,128)S(1)} %reshape.39) | data formatting | bytes 24576 | tf_op jit(solution)/shard_map/reshape | solution.py:385
  (6 shorter events, 0.1 us)
Async XLA Ops:
  0.0 0.7 %copy-start.6 = (s32[128]{0:T(128)S(1)}, s32[128]{0:T(128)}, u32[]{:S(2)}) copy-start(s32[128]{0:T(128)} %param.12) | copy-start | bytes 1540
  0.7 0.7 %copy-start.7 = (s32[128,1]{0,1:T(1,128)S(1)}, s32[128,1]{0,1:T(1,128)}, u32[]{:S(2)}) copy-start(s32[128,1]{0,1:T(1,128)} %param.10) | copy-start | bytes 1540
  1.5 0.7 %copy-start.4 = (s32[128]{0:T(128)S(1)}, s32[128]{0:T(128)}, u32[]{:S(2)}) copy-start(s32[128]{0:T(128)} %param.11) | copy-start | bytes 1540
  1.5 0.7 %copy-start.5 = (s32[128]{0:T(128)S(1)}, s32[128]{0:T(128)}, u32[]{:S(2)}) copy-start(s32[128]{0:T(128)} %param.14) | copy-start | bytes 1540
  3.3 1.6 %copy-start = (f32[128,3,384]{2,0,1:T(8,128)S(1)}, f32[128,3,384]{2,0,1:T(8,128)}, u32[]{:S(2)}) copy-start(f32[128,3,384]{2,0,1:T(8,128)} %param.13) | copy-start | bytes 1769476
  3.3 1.6 %copy-start.1 = (bf16[128,256]{1,0:T(8,128)(2,1)S(1)}, bf16[128,256]{1,0:T(8,128)(2,1)}, u32[]{:S(2)}) copy-start(bf16[128,256]{1,0:T(8,128)(2,1)} %constant.43.clone.right1) | copy-start | bytes 196612
  3.3 1.6 %copy-start.2 = (bf16[128,256]{1,0:T(8,128)(2,1)S(1)}, bf16[128,256]{1,0:T(8,128)(2,1)}, u32[]{:S(2)}) copy-start(bf16[128,256]{1,0:T(8,128)(2,1)} %constant.42.clone.right0) | copy-start | bytes 196612
  3.4 1.6 %copy-start.3 = (bf16[64,128]{1,0:T(8,128)(2,1)S(1)}, bf16[64,128]{1,0:T(8,128)(2,1)}, u32[]{:S(2)}) copy-start(bf16[64,128]{1,0:T(8,128)(2,1)} %constant.44.clone.left) | copy-start | bytes 49156

commit v4 on v3

--- a/solution.py
+++ b/solution.py
@@ -190,7 +190,9 @@
         pick(oim, -ore, ore, oim),
         pick(-ore, -oim, oim, -ore),
     ]
-    return jnp.concatenate(rows, axis=0).astype(jnp.bfloat16)
+    rows = jnp.concatenate(rows, axis=0)
+    high = rows.astype(jnp.bfloat16)
+    return jnp.concatenate([high, (rows - high.astype(jnp.float32)).astype(jnp.bfloat16)], axis=1)
 
 
 def fused_kernel(
@@ -221,6 +223,13 @@
 
     pack(0, recv)
     meta_recv[0] = meta_ref[me]
+    partial[...] = jnp.zeros_like(partial)
+
+    @pl.loop(0, blocks_ref.shape[0], step=2)
+    def _(b):
+        for i in range(2):
+            folded[b + i] = fold_one(blocks_ref[b + i], right0[...], right1[...], left[...])
+
 
     def meta_copy(d):
         return pltpu.make_async_remote_copy(
@@ -245,17 +254,12 @@
         pack(d, send)
         slot_copy(d).start()
 
-    @pl.loop(0, blocks_ref.shape[0])
-    def _(b):
-        folded[b] = fold_one(blocks_ref[b], right0[...], right1[...], left[...])
-
     @pl.loop(1, n)
     def _(d):
         meta_copy(d).wait()
 
     to_scalars = pltpu.make_async_copy(meta_recv, meta_smem, local_sem)
     to_scalars.start()
-    partial[...] = jnp.zeros_like(partial)
     to_scalars.wait()
 
     @pl.loop(0, n)
@@ -274,6 +278,7 @@
             c, s = load(rv, t), load(sv, t)
             cw, sw = cw_ref[t : t + 1, :], sw_ref[t : t + 1, :]
             basis = jnp.concatenate([c * cw, s * cw, c * sw, s * sw], axis=0).astype(jnp.bfloat16)
+            basis = jnp.concatenate([basis, basis], axis=0)
             inner = jnp.dot(folded[meta_smem[d, 0, GROUP + t]], basis, preferred_element_type=jnp.float32)
             rc, rs = load(ru, t), load(su, t)
             re = jnp.sum(rc * inner[:HALF] + rs * inner[2 * HALF : 3 * HALF], axis=0, keepdims=True)
@@ -282,22 +287,16 @@
             sums[t : t + 1, vis:] = im
         hc, hs = uc * vc - us * vs, uc * vs + us * vc
         re, im = sums[:, :vis], sums[:, vis:]
-        meta = meta_recv[d].astype(jnp.float32)
-
-        def column(first):
-            picked = jnp.where(meta_lane == meta_row + first, meta, 0.0)
-            return jnp.sum(picked, axis=1, keepdims=True)
-
-        live = lax.broadcasted_iota(jnp.int32, (GROUP, vis), 1).astype(jnp.float32) < column(0)
+        meta = meta_recv[d]
+        count = jnp.sum(jnp.where(meta_lane == meta_row, meta.astype(jnp.float32), 0.0), axis=1, keepdims=True)
+        live = lax.broadcasted_iota(jnp.int32, (GROUP, vis), 1).astype(jnp.float32) < count
         both = jnp.concatenate([re * hc - im * hs, re * hs + im * hc], axis=0)
         both = jnp.where(jnp.concatenate([live, live], axis=0), both, 0.0)
         high = both.astype(jnp.bfloat16).astype(jnp.float32)
         both = jnp.concatenate([high, both - high], axis=0).astype(jnp.bfloat16)
-        row = column(2 * GROUP)
-        row = jnp.concatenate([row, row + BL_DEV, row, row + BL_DEV], axis=0)
-        onehot = lax.broadcasted_iota(jnp.int32, (4 * GROUP, n * 2 * BL_DEV), 1).astype(jnp.float32) == row
+        onehot = lax.broadcasted_iota(jnp.int32, (n * 2 * BL_DEV, 4 * GROUP), 0) == meta[:, 4 * GROUP :]
         onehot = jnp.where(onehot, 1.0, 0.0).astype(jnp.bfloat16)
-        added = lax.dot_general(onehot, both, (((0,), (0,)), ((), ())), preferred_element_type=jnp.float32)
+        added = jnp.dot(onehot, both, preferred_element_type=jnp.float32)
         partial[...] += added.reshape(partial.shape)
 
     def share_copy(d):
@@ -335,7 +334,7 @@
             pltpu.VMEM((n, 3, GROUP, vis), jnp.int16),
             pltpu.VMEM((n, 1, META), jnp.int32),
             pltpu.SMEM((n, 1, META), jnp.int32),
-            pltpu.VMEM((blocks.shape[0], 2 * SUB, 2 * SUB), jnp.bfloat16),
+            pltpu.VMEM((blocks.shape[0], 2 * SUB, 4 * SUB), jnp.bfloat16),
             table,
             table,
             table,
@@ -376,10 +375,10 @@
     source = jnp.sum(jnp.where(hit, jnp.arange(tasks, dtype=jnp.int32)[None, :], 0), axis=1)
     if capacity == GROUP:
         row = (baseline_of_task // BL_DEV) * (2 * BL_DEV) + baseline_of_task % BL_DEV
-        meta = jnp.stack([vis_count, task_block, row])
+        none = jnp.zeros_like(row)
+        meta = jnp.stack([vis_count, task_block, none, none, row, row + BL_DEV, row, row + BL_DEV])
         meta = jnp.where(hit.reshape(facets, 1, capacity, tasks), meta[None, :, None, :], 0)
-        meta = jnp.sum(meta, axis=3).reshape(facets, 1, 3 * capacity)
-        meta = jnp.pad(meta, ((0, 0), (0, 0), (0, META - 3 * capacity)))
+        meta = jnp.sum(meta, axis=3).reshape(facets, 1, META)
         blocks = model_blocks.reshape(model_blocks.shape[0], 2 * SUB, 2 * SUB)
         share = fused(source, coords.transpose(1, 0, 2), meta, blocks, facets)
         return share.reshape(2, BL_DEV, vis).transpose(1, 0, 2)

time: 51.2 us -> 48.6 us (0.949)
  Pallas kernels: 45.4 us -> 41.5 us
  other arithmetic: 1.33 us -> 2.64 us
    pallas_call x1, Pallas kernels: 45.4 us -> 41.5 us  [fused(): pl.pallas_call(functools.partial(fused_kernel, n), out_shape=jax.ShapeDty...]
    reduce_sum x1, other arithmetic: 0.91 us -> 2.23 us  [body(): meta = jnp.sum(meta, axis=3).reshape(facets, 1, META)]
where the time goes in v4:
time: 48.6 us; the launch traced here: 48.4 us
  Pallas kernels  41.5 us (85%)
  local copies, waits for them, and re-layouts  4.13 us (8%)
  other arithmetic  2.64 us (5%)
    pallas_call x1, Pallas kernels, fused(): pl.pallas_call(functools.partial(fused_kernel, n), out_shape=jax.ShapeDty...  41.5 us
    unnamed x17, local copies, waits for them, and re-layouts  3.39 us
    reduce_sum x1, other arithmetic, body(): meta = jnp.sum(meta, axis=3).reshape(facets, 1, META)  2.23 us

profile of v4, /device:TPU:0, one launch (start us, length us, event | category | flops | bytes accessed | tf_op | source)
XLA Modules:
  0.0 48.4 jit_solution(17643496096752380973)
XLA Ops:
  0.0 0.0 copy-start.6
  0.0 0.7 %copy-done.6 = s32[128,1]{0,1:T(1,128)S(1)} copy-done((s32[128,1]{0,1:T(1,128)S(1)}, s32[128,1]{0,1:T(1,128)}, u32[]{:S(2)}) %copy-start.6) | copy-done | bytes 536
  0.7 0.2 convert_reduce_fusion
  0.8 0.0 copy-start.7
  0.9 0.1 select_reduce_fusion.1.source
  1.0 0.5 %copy-done.7 = s32[128]{0:T(128)S(1)} copy-done((s32[128]{0:T(128)S(1)}, s32[128]{0:T(128)}, u32[]{:S(2)}) %copy-start.7) | copy-done | bytes 536
  1.5 0.0 copy-start.4
  1.5 0.0 copy-start.5
  1.6 0.6 %copy-done.4 = s32[128]{0:T(128)S(1)} copy-done((s32[128]{0:T(128)S(1)}, s32[128]{0:T(128)}, u32[]{:S(2)}) %copy-start.4) | copy-done | bytes 536
  2.2 0.0 copy-done.5
  2.2 0.1 broadcast_compare_fusion
  2.3 2.2 %select_reduce_fusion = s32[16,8,16]{2,1,0:T(8,128)S(1)} fusion(s32[8,128]{1,0:T(8,128)S(1)} %stack.25, pred[16,16,128]{2,1,0:T(8,128)(4,1)S(1)} %broadcast_compare_fusion), kind=kLoop, calls=%fused_computation | loop fusion | flops 522240 | bytes 45056 | tf_op jit(solution)/shard_map/reduce_sum | solution.py:381
  4.6 0.1 reshape.37.meta_ref
  4.7 0.0 copy-start
  4.7 0.0 copy-start.1
  4.7 0.0 copy-start.2
  4.7 0.0 copy-start.3
  4.7 1.5 %copy.12 = bf16[4,8,128,128]{3,2,1,0:T(8,128)(2,1)S(1)} copy(bf16[4,8,128,128]{3,1,2,0:T(8,128)(2,1)} %bitcast.15) | data formatting | bytes 2097152
  6.2 0.0 copy-done
  6.3 0.0 copy-done.1
  6.3 0.0 copy-done.2
  6.3 0.0 copy-done.3
  6.3 41.5 %shard_map.91 = f32[8,384]{1,0:T(8,128)S(1)} custom-call(s32[256]{0:T(256)S(1)} %select_reduce_fusion.1.source, f32[3,128,384]{2,1,0:T(8,128)S(1)} %bitcast.14, s32[16,1,128]{2,1,0:T(1,128)S(1)} %reshape.37.meta_ref, bf16[32,128,128]{2,1,0:T(8,128)(2,1)S(1)} %bitcast.13, bf16[128,256]{1,0:T(8,128)(2,1)S(1)} %copy-done.2, bf16[128,256]{1,0:T(8,128)(2,1)S(1)} %copy-done.1, ...), custom_call_target="tpu_custom_call" | custom-call | flops 3221225472 | bytes 1179648 | tf_op jit(solution)/shard_map/pallas_call | solution.py:326
  47.8 0.6 %copy.14 = f32[2,4,384]{2,0,1:T(2,128)} copy(f32[2,4,384]{2,1,0:T(4,128)S(1)} %reshape.39) | data formatting | bytes 24576 | tf_op jit(solution)/shard_map/reshape | solution.py:384
  (6 shorter events, 0.1 us)
Async XLA Ops:
  0.0 0.7 %copy-start.6 = (s32[128,1]{0,1:T(1,128)S(1)}, s32[128,1]{0,1:T(1,128)}, u32[]{:S(2)}) copy-start(s32[128,1]{0,1:T(1,128)} %param.10) | copy-start | bytes 1540
  0.8 0.7 %copy-start.7 = (s32[128]{0:T(128)S(1)}, s32[128]{0:T(128)}, u32[]{:S(2)}) copy-start(s32[128]{0:T(128)} %param.12) | copy-start | bytes 1540
  1.5 0.7 %copy-start.4 = (s32[128]{0:T(128)S(1)}, s32[128]{0:T(128)}, u32[]{:S(2)}) copy-start(s32[128]{0:T(128)} %param.14) | copy-start | bytes 1540
  1.5 0.7 %copy-start.5 = (s32[128]{0:T(128)S(1)}, s32[128]{0:T(128)}, u32[]{:S(2)}) copy-start(s32[128]{0:T(128)} %param.11) | copy-start | bytes 1540
  4.7 1.6 %copy-start = (f32[128,3,384]{2,0,1:T(8,128)S(1)}, f32[128,3,384]{2,0,1:T(8,128)}, u32[]{:S(2)}) copy-start(f32[128,3,384]{2,0,1:T(8,128)} %param.13) | copy-start | bytes 1769476
  4.7 1.6 %copy-start.1 = (bf16[128,256]{1,0:T(8,128)(2,1)S(1)}, bf16[128,256]{1,0:T(8,128)(2,1)}, u32[]{:S(2)}) copy-start(bf16[128,256]{1,0:T(8,128)(2,1)} %constant.45.clone.right1) | copy-start | bytes 196612
  4.7 1.6 %copy-start.2 = (bf16[128,256]{1,0:T(8,128)(2,1)S(1)}, bf16[128,256]{1,0:T(8,128)(2,1)}, u32[]{:S(2)}) copy-start(bf16[128,256]{1,0:T(8,128)(2,1)} %constant.44.clone.right0) | copy-start | bytes 196612
  4.7 1.6 %copy-start.3 = (bf16[64,128]{1,0:T(8,128)(2,1)S(1)}, bf16[64,128]{1,0:T(8,128)(2,1)}, u32[]{:S(2)}) copy-start(bf16[64,128]{1,0:T(8,128)(2,1)} %constant.46.clone.left) | copy-start | bytes 49156

commit v5 on v4

--- a/solution.py
+++ b/solution.py
@@ -15,7 +15,7 @@
 BL_DEV = 4
 GROUP = 16
 META = 128
-PITCH = 40
+PITCH = 33
 STEPS = 16383.5
 MESH = pl.DeviceIdType.MESH
 
@@ -124,7 +124,7 @@
 def compute(slots, block_ids, baselines, folded, n_baselines, vis):
     n, width = slots.shape
     lanes = vis // 128
-    table = pltpu.VMEM((lanes, GROUP * PITCH, 128), jnp.float32)
+    table = pltpu.VMEM((lanes, (GROUP + 1) * PITCH, 128), jnp.float32)
     return pl.pallas_call(
         compute_kernel,
         out_shape=jax.ShapeDtypeStruct((n_baselines, 2 * vis), jnp.float32),
@@ -225,9 +225,9 @@
     meta_recv[0] = meta_ref[me]
     partial[...] = jnp.zeros_like(partial)
 
-    @pl.loop(0, blocks_ref.shape[0], step=2)
+    @pl.loop(0, blocks_ref.shape[0], step=8)
     def _(b):
-        for i in range(2):
+        for i in range(8):
             folded[b + i] = fold_one(blocks_ref[b + i], right0[...], right1[...], left[...])
 
 
@@ -319,7 +319,7 @@
 
 def fused(source, coords, meta, blocks, n):
     vis = coords.shape[2]
-    table = pltpu.VMEM((vis // 128, GROUP * PITCH, 128), jnp.float32)
+    table = pltpu.VMEM((vis // 128, (GROUP + 1) * PITCH, 128), jnp.float32)
     vmem = pl.BlockSpec(memory_space=pltpu.VMEM)
     rows = 2 * BL_DEV
     sems = pltpu.SemaphoreType.DMA((n,))

time: 48.6 us -> 43.9 us (0.903)
  Pallas kernels: 41.5 us -> 36.8 us
    pallas_call x1, Pallas kernels: 41.5 us -> 36.8 us  [fused(): pl.pallas_call(functools.partial(fused_kernel, n), out_shape=jax.ShapeDty...]
where the time goes in v5:
time: 43.9 us; the launch traced here: 43.8 us
  Pallas kernels  36.8 us (84%)
  local copies, waits for them, and re-layouts  4.13 us (9%)
  other arithmetic  2.64 us (6%)
    pallas_call x1, Pallas kernels, fused(): pl.pallas_call(functools.partial(fused_kernel, n), out_shape=jax.ShapeDty...  36.8 us
    unnamed x17, local copies, waits for them, and re-layouts  3.39 us
    reduce_sum x1, other arithmetic, body(): meta = jnp.sum(meta, axis=3).reshape(facets, 1, META)  2.23 us

profile of v5, /device:TPU:0, one launch (start us, length us, event | category | flops | bytes accessed | tf_op | source)
XLA Modules:
  0.0 43.8 jit_solution(3159627861158541389)
XLA Ops:
  0.0 0.0 copy-start.6
  0.0 0.7 %copy-done.6 = s32[128,1]{0,1:T(1,128)S(1)} copy-done((s32[128,1]{0,1:T(1,128)S(1)}, s32[128,1]{0,1:T(1,128)}, u32[]{:S(2)}) %copy-start.6) | copy-done | bytes 536
  0.7 0.2 convert_reduce_fusion
  0.8 0.0 copy-start.7
  0.9 0.1 select_reduce_fusion.1.source
  1.0 0.5 %copy-done.7 = s32[128]{0:T(128)S(1)} copy-done((s32[128]{0:T(128)S(1)}, s32[128]{0:T(128)}, u32[]{:S(2)}) %copy-start.7) | copy-done | bytes 536
  1.5 0.0 copy-start.4
  1.5 0.0 copy-start.5
  1.6 0.6 %copy-done.4 = s32[128]{0:T(128)S(1)} copy-done((s32[128]{0:T(128)S(1)}, s32[128]{0:T(128)}, u32[]{:S(2)}) %copy-start.4) | copy-done | bytes 536
  2.2 0.0 copy-done.5
  2.2 0.1 broadcast_compare_fusion
  2.3 2.2 %select_reduce_fusion = s32[16,8,16]{2,1,0:T(8,128)S(1)} fusion(s32[8,128]{1,0:T(8,128)S(1)} %stack.25, pred[16,16,128]{2,1,0:T(8,128)(4,1)S(1)} %broadcast_compare_fusion), kind=kLoop, calls=%fused_computation | loop fusion | flops 522240 | bytes 45056 | tf_op jit(solution)/shard_map/reduce_sum | solution.py:381
  4.6 0.1 reshape.37.meta_ref
  4.7 0.0 copy-start
  4.7 0.0 copy-start.1
  4.7 0.0 copy-start.2
  4.7 0.0 copy-start.3
  4.7 1.5 %copy.12 = bf16[4,8,128,128]{3,2,1,0:T(8,128)(2,1)S(1)} copy(bf16[4,8,128,128]{3,1,2,0:T(8,128)(2,1)} %bitcast.15) | data formatting | bytes 2097152
  6.2 0.0 copy-done
  6.3 0.0 copy-done.1
  6.3 0.0 copy-done.2
  6.3 0.0 copy-done.3
  6.3 36.8 %shard_map.91 = f32[8,384]{1,0:T(8,128)S(1)} custom-call(s32[256]{0:T(256)S(1)} %select_reduce_fusion.1.source, f32[3,128,384]{2,1,0:T(8,128)S(1)} %bitcast.14, s32[16,1,128]{2,1,0:T(1,128)S(1)} %reshape.37.meta_ref, bf16[32,128,128]{2,1,0:T(8,128)(2,1)S(1)} %bitcast.13, bf16[128,256]{1,0:T(8,128)(2,1)S(1)} %copy-done.2, bf16[128,256]{1,0:T(8,128)(2,1)S(1)} %copy-done.1, ...), custom_call_target="tpu_custom_call" | custom-call | flops 3221225472 | bytes 1179648 | tf_op jit(solution)/shard_map/pallas_call | solution.py:326
  43.2 0.6 %copy.14 = f32[2,4,384]{2,0,1:T(2,128)} copy(f32[2,4,384]{2,1,0:T(4,128)S(1)} %reshape.39) | data formatting | bytes 24576 | tf_op jit(solution)/shard_map/reshape | solution.py:384
  (6 shorter events, 0.1 us)
Async XLA Ops:
  0.0 0.7 %copy-start.6 = (s32[128,1]{0,1:T(1,128)S(1)}, s32[128,1]{0,1:T(1,128)}, u32[]{:S(2)}) copy-start(s32[128,1]{0,1:T(1,128)} %param.10) | copy-start | bytes 1540
  0.8 0.7 %copy-start.7 = (s32[128]{0:T(128)S(1)}, s32[128]{0:T(128)}, u32[]{:S(2)}) copy-start(s32[128]{0:T(128)} %param.12) | copy-start | bytes 1540
  1.5 0.7 %copy-start.4 = (s32[128]{0:T(128)S(1)}, s32[128]{0:T(128)}, u32[]{:S(2)}) copy-start(s32[128]{0:T(128)} %param.14) | copy-start | bytes 1540
  1.5 0.7 %copy-start.5 = (s32[128]{0:T(128)S(1)}, s32[128]{0:T(128)}, u32[]{:S(2)}) copy-start(s32[128]{0:T(128)} %param.11) | copy-start | bytes 1540
  4.7 1.6 %copy-start = (f32[128,3,384]{2,0,1:T(8,128)S(1)}, f32[128,3,384]{2,0,1:T(8,128)}, u32[]{:S(2)}) copy-start(f32[128,3,384]{2,0,1:T(8,128)} %param.13) | copy-start | bytes 1769476
  4.7 1.6 %copy-start.1 = (bf16[128,256]{1,0:T(8,128)(2,1)S(1)}, bf16[128,256]{1,0:T(8,128)(2,1)}, u32[]{:S(2)}) copy-start(bf16[128,256]{1,0:T(8,128)(2,1)} %constant.45.clone.right1) | copy-start | bytes 196612
  4.7 1.6 %copy-start.2 = (bf16[128,256]{1,0:T(8,128)(2,1)S(1)}, bf16[128,256]{1,0:T(8,128)(2,1)}, u32[]{:S(2)}) copy-start(bf16[128,256]{1,0:T(8,128)(2,1)} %constant.44.clone.right0) | copy-start | bytes 196612
  4.7 1.6 %copy-start.3 = (bf16[64,128]{1,0:T(8,128)(2,1)S(1)}, bf16[64,128]{1,0:T(8,128)(2,1)}, u32[]{:S(2)}) copy-start(bf16[64,128]{1,0:T(8,128)(2,1)} %constant.46.clone.left) | copy-start | bytes 49156
